TPU v7x, 32 devices: a whole 2x2x4 slice. The times are simulated.
32 devices in a mesh: prow: 4 (over y, core), pcol: 8 (over z, x).
Axes of the slice: x: 2, y: 2, z: 4, core: 2. Of those that a mesh axis runs over, the one named last changes fastest.
Arguments:
- trailing: float32 [8, 4, 128, 4, 8, 128], P(None, 'prow', None, None, 'pcol'), may hold values from -8 to 8, as said below
- reflectors: float32 [8, 4, 128, 256], P(None, 'prow', None, 'pcol'), may hold values from -0.5 to 0.5
- tfactor: float32 [256, 256], replicated, may hold values from -0.375 to 0.375
Outputs:
- updated: float32 [8, 4, 128, 4, 8, 128], P(None, 'prow', None, None, 'pcol')
Inputs may be any that keep to these rules, and one draw needn't show every extreme that they name: trailing is symmetric as a matrix of order 4096.
All inputs are finite; a program needn't handle non-finite values.
Results may differ from a plain program's by a relative error of at most 0.00011.
Values sent between devices are 32-bit elements; how exact they have to be, the bound alone decides.
No kernel may reach another device: no remote copies, remote signals or barrier semaphores. Data moves between devices by JAX's collectives and lax.ppermute only.
A program may use at most 64 MiB of HBM per device.

v0:
```python
import functools

import jax
import jax.numpy as jnp
from jax import lax
from jax.experimental import pallas as pl
from jax.experimental.pallas import tpu as pltpu
from jax.sharding import PartitionSpec as P

BOTH = ("prow", "pcol")
F32 = jnp.float32
BF16 = jnp.bfloat16
VMEM = pltpu.CompilerParams(vmem_limit_bytes=8 * 1024 * 1024)


def split(values):
    high = values.astype(BF16)
    return high, (values - high.astype(F32)).astype(BF16)


def dot(left, right, dims=((1,), (0,))):
    return lax.dot_general(left, right, (dims, ((), ())), preferred_element_type=F32)


def dot3(left, right, dims=((1,), (0,))):
    (lh, ll), (rh, rl) = left, right
    return dot(lh, rh, dims) + (dot(lh, rl, dims) + dot(ll, rh, dims))


def swap(values, axis, mask):
    n = lax.axis_size(axis)
    return lax.ppermute(values, axis, [(i, i ^ mask) for i in range(n)])


def halving(n):
    masks = []
    while n > 1:
        n //= 2
        masks.append(n)
    return masks


def join(values, other, high):
    pair = jnp.stack([jnp.where(high, other, values), jnp.where(high, values, other)])
    return pair.reshape((-1,) + values.shape[1:])


def gather(values, axis, masks, above):
    values = values[None]
    for mask in masks:
        values = join(values, swap(values, axis, mask), above[mask])
    return values


def slot(index, masks):
    return sum(1 << j for j, mask in enumerate(masks) if index & mask)


def swap_three(values, axis):
    return [swap(values, axis, mask) for mask in (1, 2, 3)]


def split_block_kernel(col_tiles, tile, a_ref, high_ref, low_ref):
    rows = high_ref.shape[0]
    for b in range(col_tiles):
        cols = slice(b * tile, (b + 1) * tile)
        high, low = split(a_ref[pl.ds(b, rows, stride=col_tiles), :])
        high_ref[:, cols] = high
        low_ref[:, cols] = low


def product_kernel(orders, ah_ref, al_ref, first_ref, second_ref, y_ref, keep_ref, send_ref, yh, yl, total):
    nc, half, width, tile = first_ref.shape
    for chunk, (ref, masks) in enumerate(zip((first_ref, second_ref), orders)):
        for a in range(half):
            at = chunk * half + a
            for j in range(nc):
                y_ref[at, j * width : (j + 1) * width, :] = ref[slot(j, masks), a]
            cols = slice(at * tile, (at + 1) * tile)
            yh[:, cols], yl[:, cols] = split(y_ref[at])
    total[...] = dot3((yh[...], yl[...]), (ah_ref[...], al_ref[...]))
    core = lax.axis_index("prow") & 1
    count, part = keep_ref.shape[:2]
    for y in range(count):
        keep_ref[y] = total[pl.ds(pl.multiple_of((2 * y + core) * part, part), part), :]
        send_ref[y] = total[pl.ds(pl.multiple_of((2 * y + 1 - core) * part, part), part), :]


def inner_kernel(shift, piece_ref, y_ref, inner_ref):
    row_tiles, nb, tile = y_ref.shape
    part, cols = piece_ref.shape
    col_tiles = cols // tile
    half = part // 2
    group = lax.axis_index("pcol") >> shift
    inner = jnp.zeros((part, nb), F32)
    for b in range(col_tiles):
        left = split(piece_ref[:, b * tile : (b + 1) * tile])
        inner += dot3(left, split(y_ref[b * (row_tiles // col_tiles) + group]), ((1,), (1,)))
    for side in range(2):
        inner_ref[:, side * nb : (side + 1) * nb] = inner[side * half : (side + 1) * half]


def row_factor_kernel(t_ref, y_ref, high_ref, low_ref):
    row_tiles, nb, tile = y_ref.shape
    factor = split(t_ref[...])
    for a in range(row_tiles):
        rows = slice(a * tile, (a + 1) * tile)
        high_ref[rows, :], low_ref[rows, :] = split(dot3(factor, split(y_ref[a])).T)


def column_factor_kernel(order, t_ref, cols_ref, high_ref, low_ref, z_ref, y):
    slots, _, half, _ = cols_ref.shape
    for s in range(slots):
        for side in range(2):
            rows = slice((2 * s + side) * half, (2 * s + side + 1) * half)
            z_ref[rows, :] = cols_ref[slot(s, order), side]
            y[rows, :] = cols_ref[slot(s, order), 2 + side]
    high_ref[...], low_ref[...] = split(dot3(split(t_ref[...]), split(y[...])))


def update_kernel(
    orders, inner_upper, a_ref, urh_ref, url_ref, uch_ref, ucl_ref, zc_ref, first_ref, second_ref, *refs
):
    inners, (out_ref, inner, zt, block, result, read, write) = refs[:4], refs[4:]
    near = lax.axis_index("pcol") & 3
    ratio, nb, cols = zt.shape
    nc, half = first_ref.shape[:2]
    slots = nc // ratio
    chunks, lines, tile = block.shape
    col_tiles = cols // tile
    reads = [pltpu.make_async_copy(a_ref.at[pl.ds(i * lines, lines)], block.at[i], read.at[i]) for i in range(chunks)]
    writes = [pltpu.make_async_copy(result.at[i], out_ref.at[pl.ds(i * lines, lines)], write.at[i]) for i in range(chunks)]
    for copy in reads:
        copy.start()
    for g in range(ratio):
        for s in range(slots):
            for side, (ref, masks) in enumerate(zip((first_ref, second_ref), orders)):
                at = (2 * s + side) * half
                zt[g, at : at + half, :] = ref[slot(g * slots + s, masks)]
    for r in range(4):
        for u in range(slots // 4):
            for side in range(2):
                at = pl.multiple_of((2 * (u * 4 + (near ^ r)) + side) * half, half)
                inner[pl.ds(at, half), :] = inners[r][slot(u, inner_upper), :, side * nb : (side + 1) * nb]
    uc = (uch_ref[...], ucl_ref[...])
    w = split(zc_ref[...] - dot3(split(inner[...]), uc))
    rows = lines // col_tiles
    count = rows // (ratio * tile)
    for i in range(chunks):
        at = slice(i * rows, (i + 1) * rows)
        turned = [zt[g, :, b * tile : (b + 1) * tile].T for b in range(i * count, (i + 1) * count) for g in range(ratio)]
        total = dot3(split(jnp.concatenate(turned, axis=0)), uc) + dot3((urh_ref[at, :], url_ref[at, :]), w)
        reads[i].wait()
        for g in range(ratio * count):
            for b in range(col_tiles):
                line = pl.ds(g * tile * col_tiles + b, tile, stride=col_tiles)
                result[i, line, :] = block[i, line, :] - total[g * tile : (g + 1) * tile, b * tile : (b + 1) * tile]
        writes[i].start()
    for copy in writes:
        copy.wait()


def shape(*dims, dtype=F32):
    return jax.ShapeDtypeStruct(dims, dtype)


def per_device(trailing, reflectors, tfactor):
    row_tiles, _, tile, col_tiles = trailing.shape[:4]
    np_, nc = lax.axis_size("prow"), lax.axis_size("pcol")
    ratio = nc // np_
    ny = np_ // 2
    rows, cols = row_tiles * tile, col_tiles * tile
    nb = tfactor.shape[0]
    part = nb // np_
    half = row_tiles // 2
    block = trailing.reshape(rows * col_tiles, tile)
    mine = jnp.transpose(reflectors.reshape(row_tiles, tile, -1), (0, 2, 1))

    masks, cols_order = halving(nc), halving(np_)
    lead, rest = masks[: len(masks) - len(cols_order)], masks[len(masks) - len(cols_order) :]
    shift = len(cols_order)
    prow, pcol = lax.axis_index("prow").astype(jnp.int32), lax.axis_index("pcol").astype(jnp.int32)
    group = pcol >> shift
    where = {
        "group": group,
        "share": (pcol & (np_ - 1)) * part,
        "col": {mask: (pcol & mask) != 0 for mask in masks},
        "row": {mask: (prow & mask) != 0 for mask in cols_order},
        "half": {mask: [jnp.where((prow & mask) != 0, 1 - side, side) for side in range(2)] for mask in cols_order},
    }
    mine, where = lax.optimization_barrier((mine, where))
    group, col, row = where["group"], where["col"], where["row"]
    whole = pl.BlockSpec(memory_space=pltpu.VMEM)

    def flat(p, q):
        return p * nc + q

    def turn(values):
        perm = [
            (flat(p, g * np_ + s), flat(s, g * np_ + p)) for p in range(np_) for g in range(ratio) for s in range(np_)
        ]
        return lax.ppermute(values, BOTH, perm)

    inner_upper = [mask // 4 for mask in rest[:-2]]
    far, close = rest[-2:]
    orders = (masks, masks[:-2] + [close, far])
    a_high, a_low = pl.pallas_call(
        functools.partial(split_block_kernel, col_tiles, tile),
        out_shape=[shape(rows, cols, dtype=BF16)] * 2,
        in_specs=[whole],
        out_specs=[whole] * 2,
        compiler_params=VMEM,
        cost_estimate=pl.CostEstimate(flops=rows * cols * 4, bytes_accessed=rows * cols * 8, transcendentals=0),
    )(block)
    first, second = lax.optimization_barrier(mine[None, :half]), lax.optimization_barrier(mine[None, half:])
    for at, (mask, other) in enumerate(zip(*orders)):
        first_came, second_came = swap(first, "pcol", mask), swap(second, "pcol", other)
        if at == 0:
            second_came, a_high, a_low = lax.optimization_barrier((second_came, a_high, a_low))
        first, second = join(first, first_came, col[mask]), join(second, second_came, col[other])

    y_rows, keep, send = pl.pallas_call(
        functools.partial(product_kernel, orders),
        out_shape=[shape(row_tiles, nb, tile), shape(ny, part, cols), shape(ny, part, cols)],
        in_specs=[whole] * 4,
        out_specs=[whole] * 3,
        scratch_shapes=[pltpu.VMEM((nb, rows), BF16), pltpu.VMEM((nb, rows), BF16), pltpu.VMEM((nb, cols), F32)],
        compiler_params=VMEM,
        cost_estimate=pl.CostEstimate(flops=6 * nb * rows * cols, bytes_accessed=rows * cols * 8, transcendentals=0),
    )(a_high, a_low, first, second)
    other = swap(send, "prow", 1)
    kept = keep + other
    y_piece = lax.dynamic_slice(
        y_rows.reshape(col_tiles, ratio, nb, tile), (0, group, where["share"], 0), (col_tiles, 1, part, tile)
    )
    y_piece = jnp.transpose(y_piece.reshape(col_tiles, part, tile), (1, 0, 2)).reshape(part, cols)
    for mask in cols_order[:-1]:
        low, high = where["half"][mask]
        pair = kept.reshape(2, mask // 2, part, cols)
        kept = lax.dynamic_index_in_dim(pair, low, 0, keepdims=False)
        kept = kept + swap(lax.dynamic_index_in_dim(pair, high, 0, keepdims=False), "prow", mask)
    piece = kept.reshape(part, cols)

    turned = turn(piece)
    y_cols = turn(y_piece).reshape(2, part // 2, cols)
    urh, url = pl.pallas_call(
        row_factor_kernel,
        out_shape=[shape(rows, nb, dtype=BF16)] * 2,
        in_specs=[whole] * 2,
        out_specs=[whole] * 2,
        compiler_params=VMEM,
        cost_estimate=pl.CostEstimate(flops=6 * nb * nb * rows, bytes_accessed=rows * nb * 8, transcendentals=0),
    )(tfactor, y_rows)
    turned, urh, url = lax.optimization_barrier((turned, urh, url))
    inner = pl.pallas_call(
        functools.partial(inner_kernel, shift),
        out_shape=shape(part // 2, 2 * nb),
        in_specs=[whole] * 2,
        out_specs=whole,
        compiler_params=VMEM,
        cost_estimate=pl.CostEstimate(flops=6 * nb * part * cols, bytes_accessed=cols * nb * 4, transcendentals=0),
    )(turned, y_rows)
    first, second = turned[None, : part // 2], turned[None, part // 2 :]
    first, second = lax.optimization_barrier(first), lax.optimization_barrier(second)
    for mask in lead + rest[:-2]:
        first = join(first, swap(first, "pcol", mask), col[mask])
        second = join(second, swap(second, "pcol", mask), col[mask])
    first = join(first, swap(first, "pcol", far), col[far])
    second = join(second, swap(second, "pcol", close), col[close])

    columns = jnp.concatenate([piece.reshape(2, part // 2, cols), y_cols])
    for mask in cols_order[::-1]:
        inner = inner + swap(inner, "prow", mask)
        if mask == 1:
            columns, inner = lax.optimization_barrier((columns, inner))
    for mask in lead:
        inner = inner + swap(inner, "pcol", mask)
    inner = inner[None]
    for mask in rest[:-2]:
        inner = join(inner, swap(inner, "pcol", mask), col[mask])
    first_came = swap(jnp.concatenate([first, inner]), "pcol", close)
    second_came = swap(jnp.concatenate([second, inner]), "pcol", far)
    blocks = first.shape[0]
    near_inner = [inner, first_came[blocks:], second_came[blocks:], swap(inner, "pcol", close + far)]
    first = join(first, first_came[:blocks], col[close])
    second = join(second, second_came[:blocks], col[far])

    columns = gather(columns, "prow", cols_order, row)
    uch, ucl, zc = pl.pallas_call(
        functools.partial(column_factor_kernel, cols_order),
        out_shape=[shape(nb, cols, dtype=BF16)] * 2 + [shape(nb, cols)],
        in_specs=[whole] * 2,
        out_specs=[whole] * 3,
        scratch_shapes=[pltpu.VMEM((nb, cols), F32)],
        compiler_params=VMEM,
        cost_estimate=pl.CostEstimate(flops=6 * nb * nb * cols, bytes_accessed=cols * nb * 8, transcendentals=0),
    )(tfactor, columns)

    chunks = 4
    lines = rows * col_tiles // chunks
    outside = pl.BlockSpec(memory_space=pltpu.HBM)
    result = pl.pallas_call(
        functools.partial(update_kernel, orders, inner_upper),
        out_shape=shape(rows * col_tiles, tile),
        in_specs=[outside] + [whole] * 11,
        out_specs=outside,
        scratch_shapes=[
            pltpu.VMEM((nb, nb), F32),
            pltpu.VMEM((ratio, nb, cols), F32),
            pltpu.VMEM((chunks, lines, tile), F32),
            pltpu.VMEM((chunks, lines, tile), F32),
            pltpu.SemaphoreType.DMA((chunks,)),
            pltpu.SemaphoreType.DMA((chunks,)),
        ],
        compiler_params=VMEM,
        cost_estimate=pl.CostEstimate(flops=12 * nb * rows * cols, bytes_accessed=rows * cols * 8, transcendentals=0),
    )(block, urh, url, uch, ucl, zc, first, second, *near_inner)
    return result.reshape(trailing.shape)


def solution(mesh):
    return jax.shard_map(
        per_device,
        mesh=mesh,
        in_specs=(P(None, "prow", None, None, "pcol", None), P(None, "prow", None, "pcol"), P()),
        out_specs=P(None, "prow", None, None, "pcol", None),
        check_vma=False,
    )
```

profile of v0, /device:TPU:0, one launch (start us, length us, event | category | flops | bytes accessed | tf_op | source)
XLA Modules:
  0.0 75.8 jit_solution(9457555648458459088)
XLA Ops:
  0.0 0.9 %slice_bitcast_fusion.2 = (f32[1,4,32,128]{3,2,1,0:T(8,128)S(1)}, f32[1,4,32,128]{3,2,1,0:T(8,128)S(1)}) fusion(f32[8,32,128]{2,1,0:T(8,128)} %bitcast.154), kind=kLoop, calls=%fused_computation.51 | loop fusion | bytes 262144 | tf_op jit(solution)/shard_map/broadcast_in_dim | solution.py:215
  0.9 4.1 %collective-permute-start.1 = (f32[1,4,32,128]{3,2,1,0:T(8,128)S(1)}, f32[1,4,32,128]{3,2,1,0:T(8,128)S(1)}, u32[]{:S(2)}, u32[]{:S(2)}) collective-permute-start(f32[1,4,32,128]{3,2,1,0:T(8,128)S(1)} %get-tuple-element.91), channel_id=1, source_target_pairs={{0,4},{1,5},{2,6},{3,7},{4,0},{5,1},{6,2},{7,3},{8,12},{9,13},{10,... | collective-permute-start | bytes 196616 | tf_op jit(solution)/shard_map/ppermute | solution.py:32
  5.0 0.1 collective-permute-start
  5.1 0.0 copy-start
  5.1 1.6 %copy-done = f32[8,1,128,4,1,128]{5,4,3,2,1,0:T(1,128)S(1)} copy-done((f32[8,1,128,4,1,128]{5,4,3,2,1,0:T(1,128)S(1)}, f32[8,1,128,4,1,128]{5,4,3,2,1,0:T(1,128)}, u32[]{:S(2)}) %copy-start) | copy-done | bytes 2097176
  6.7 0.5 shard_map.37
  7.2 1.5 %collective-permute-done.1 = f32[1,4,32,128]{3,2,1,0:T(8,128)S(1)} collective-permute-done((f32[1,4,32,128]{3,2,1,0:T(8,128)S(1)}, f32[1,4,32,128]{3,2,1,0:T(8,128)S(1)}, u32[]{:S(2)}, u32[]{:S(2)}) %collective-permute-start.1) | collective-permute-done | bytes 65568 | tf_op jit(solution)/shard_map/ppermute | solution.py:32
  8.7 2.1 %collective-permute-start.2 = (f32[2,4,32,128]{3,2,1,0:T(8,128)S(1)}, f32[2,4,32,128]{3,2,1,0:T(8,128)S(1)}, u32[]{:S(2)}, u32[]{:S(2)}) collective-permute-start(f32[2,4,32,128]{3,2,1,0:T(8,128)S(1)} %maximum_bitcast_fusion.1), channel_id=1, source_target_pairs={{0,2},{1,3},{2,0},{3,1},{4,6},{5,7},{6,4},{7,5},{8,10},{9,11},{10,... | collective-permute-start | bytes 393224 | tf_op jit(solution)/shard_map/ppermute | solution.py:32
  10.8 0.6 collective-permute-done
  11.5 1.8 %collective-permute-start.4 = (f32[2,4,32,128]{3,2,1,0:T(8,128)S(1)}, f32[2,4,32,128]{3,2,1,0:T(8,128)S(1)}, u32[]{:S(2)}, u32[]{:S(2)}) collective-permute-start(f32[2,4,32,128]{3,2,1,0:T(8,128)S(1)} %maximum_bitcast_fusion.2), channel_id=1, source_target_pairs={{0,1},{1,0},{2,3},{3,2},{4,5},{5,4},{6,7},{7,6},{8,9},{9,8},{10,11... | collective-permute-start | bytes 393224 | tf_op jit(solution)/shard_map/ppermute | solution.py:32
  13.2 1.1 %collective-permute-done.2 = f32[2,4,32,128]{3,2,1,0:T(8,128)S(1)} collective-permute-done((f32[2,4,32,128]{3,2,1,0:T(8,128)S(1)}, f32[2,4,32,128]{3,2,1,0:T(8,128)S(1)}, u32[]{:S(2)}, u32[]{:S(2)}) %collective-permute-start.2) | collective-permute-done | bytes 131104 | tf_op jit(solution)/shard_map/ppermute | solution.py:32
  14.4 1.6 %collective-permute-start.3 = (f32[4,4,32,128]{3,2,1,0:T(8,128)S(1)}, f32[4,4,32,128]{3,2,1,0:T(8,128)S(1)}, u32[]{:S(2)}, u32[]{:S(2)}) collective-permute-start(f32[4,4,32,128]{3,2,1,0:T(8,128)S(1)} %bitcast.150), channel_id=1, source_target_pairs={{0,1},{1,0},{2,3},{3,2},{4,5},{5,4},{6,7},{7,6},{8,9},{9,8},{10,11... | collective-permute-start | bytes 786440 | tf_op jit(solution)/shard_map/ppermute | solution.py:32
  16.1 0.8 %collective-permute-done.4 = f32[2,4,32,128]{3,2,1,0:T(8,128)S(1)} collective-permute-done((f32[2,4,32,128]{3,2,1,0:T(8,128)S(1)}, f32[2,4,32,128]{3,2,1,0:T(8,128)S(1)}, u32[]{:S(2)}, u32[]{:S(2)}) %collective-permute-start.4) | collective-permute-done | bytes 131104 | tf_op jit(solution)/shard_map/ppermute | solution.py:32
  17.0 0.9 %collective-permute-start.5 = (f32[4,4,32,128]{3,2,1,0:T(8,128)S(1)}, f32[4,4,32,128]{3,2,1,0:T(8,128)S(1)}, u32[]{:S(2)}, u32[]{:S(2)}) collective-permute-start(f32[4,4,32,128]{3,2,1,0:T(8,128)S(1)} %bitcast.151), channel_id=1, source_target_pairs={{0,2},{1,3},{2,0},{3,1},{4,6},{5,7},{6,4},{7,5},{8,10},{9,11},{10,... | collective-permute-start | bytes 786440 | tf_op jit(solution)/shard_map/ppermute | solution.py:32
  17.9 4.5 %collective-permute-done.3 = f32[4,4,32,128]{3,2,1,0:T(8,128)S(1)} collective-permute-done((f32[4,4,32,128]{3,2,1,0:T(8,128)S(1)}, f32[4,4,32,128]{3,2,1,0:T(8,128)S(1)}, u32[]{:S(2)}, u32[]{:S(2)}) %collective-permute-start.3) | collective-permute-done | bytes 262176 | tf_op jit(solution)/shard_map/ppermute | solution.py:32
  22.3 0.1 select_bitcast_fusion.11
  22.4 1.5 %collective-permute-done.5 = f32[4,4,32,128]{3,2,1,0:T(8,128)S(1)} collective-permute-done((f32[4,4,32,128]{3,2,1,0:T(8,128)S(1)}, f32[4,4,32,128]{3,2,1,0:T(8,128)S(1)}, u32[]{:S(2)}, u32[]{:S(2)}) %collective-permute-start.5) | collective-permute-done | bytes 262176 | tf_op jit(solution)/shard_map/ppermute | solution.py:32
  24.0 0.0 copy-start.2
  24.0 1.1 %shard_map.38 = (f32[8,256,128]{2,1,0:T(8,128)S(1)}, f32[2,64,512]{2,1,0:T(8,128)S(1)}, f32[2,64,512]{2,1,0:T(8,128)S(1)}) custom-call(bf16[1024,512]{1,0:T(8,128)(2,1)S(1)} %get-tuple-element.36.ah_ref, bf16[1024,512]{1,0:T(8,128)(2,1)S(1)} %get-tuple-element.37.al_ref, f32[8,4,32,128]{3,2,1,0:T(8,128)S(1)} %bitcast.142, f32[8,4,32,128]{3,2,1,0:T(8,128)S(1)} %bitcast.143), custom_call_target="tpu_custom_call" | custom-call | flops 805306368 | bytes 4194304 | tf_op jit(solution)/shard_map/pallas_call | solution.py:222
  25.1 0.1 collective-permute-start.6
  25.2 1.5 %collective-permute-done.6 = f32[2,64,512]{2,1,0:T(8,128)S(1)} collective-permute-done((f32[2,64,512]{2,1,0:T(8,128)S(1)}, f32[2,64,512]{2,1,0:T(8,128)S(1)}, u32[]{:S(2)}, u32[]{:S(2)}) %collective-permute-start.6) | collective-permute-done | bytes 262176 | tf_op jit(solution)/shard_map/ppermute | solution.py:32
  26.8 1.9 %collective-permute-start.7 = (f32[1,64,512]{2,1,0:T(8,128)S(1)}, f32[1,64,512]{2,1,0:T(8,128)S(1)}, u32[]{:S(2)}, u32[]{:S(2)}) collective-permute-start(f32[1,64,512]{2,1,0:T(8,128)S(1)} %constant_dynamic-slice_fusion), channel_id=1, source_target_pairs={{0,16},{8,24},{16,0},{24,8},{1,17},{9,25},{17,1},{25,9},{2,18},{10... | collective-permute-start | bytes 393224 | tf_op jit(solution)/shard_map/ppermute | solution.py:32
  28.7 3.8 %collective-permute-done.7 = f32[1,64,512]{2,1,0:T(8,128)S(1)} collective-permute-done((f32[1,64,512]{2,1,0:T(8,128)S(1)}, f32[1,64,512]{2,1,0:T(8,128)S(1)}, u32[]{:S(2)}, u32[]{:S(2)}) %collective-permute-start.7) | collective-permute-done | bytes 131104 | tf_op jit(solution)/shard_map/ppermute | solution.py:32
  32.5 0.7 collective-permute-start.8
  33.2 0.7 collective-permute-start.9
  33.9 0.0 copy-done.2
  33.9 1.0 %shard_map.39 = (bf16[1024,256]{1,0:T(8,128)(2,1)S(1)}, bf16[1024,256]{1,0:T(8,128)(2,1)S(1)}) custom-call(f32[256,256]{1,0:T(8,128)S(1)} %copy-done.2, f32[8,256,128]{2,1,0:T(8,128)S(1)} %get-tuple-element.46.y_ref), custom_call_target="tpu_custom_call" | custom-call | flops 402653184 | bytes 2097152 | tf_op jit(solution)/shard_map/pallas_call | solution.py:246
  35.0 0.0 collective-permute-done.8.piece_ref
  35.0 0.4 shard_map.40
  35.4 4.4 %collective-permute-start.10 = (f32[32,512]{1,0:T(8,128)S(1)}, f32[32,512]{1,0:T(8,128)S(1)}, u32[]{:S(2)}, u32[]{:S(2)}) collective-permute-start(f32[32,512]{1,0:T(8,128)S(1)} %shard_map.40), channel_id=1, source_target_pairs={{0,8},{8,0},{16,24},{24,16},{1,9},{9,1},{17,25},{25,17},{2,10},{10... | collective-permute-start | bytes 196616 | tf_op jit(solution)/shard_map/ppermute | solution.py:32
  39.8 2.4 %collective-permute-start.13 = (f32[1,32,512]{2,1,0:T(8,128)S(1)}, f32[1,32,512]{2,1,0:T(8,128)S(1)}, u32[]{:S(2)}, u32[]{:S(2)}) collective-permute-start(f32[1,32,512]{2,1,0:T(8,128)S(1)} %get-tuple-element.84), channel_id=1, source_target_pairs={{0,4},{1,5},{2,6},{3,7},{4,0},{5,1},{6,2},{7,3},{8,12},{9,13},{10,... | collective-permute-start | bytes 196616 | tf_op jit(solution)/shard_map/ppermute | solution.py:32
  42.2 0.0 collective-permute-done.9
  42.3 0.6 collective-permute-start.18
  42.9 0.0 collective-permute-done.10
  42.9 6.7 %collective-permute-start.15 = (f32[32,512]{1,0:T(8,128)S(1)}, f32[32,512]{1,0:T(8,128)S(1)}, u32[]{:S(2)}, u32[]{:S(2)}) collective-permute-start(f32[32,512]{1,0:T(8,128)S(1)} %add.34), channel_id=1, source_target_pairs={{0,16},{8,24},{16,0},{24,8},{1,17},{9,25},{17,1},{25,9},{2,18},{10... | collective-permute-start | bytes 196616 | tf_op jit(solution)/shard_map/ppermute | solution.py:32
  49.6 0.0 collective-permute-done.13
  49.6 0.2 collective-permute-start.14
  49.9 0.0 collective-permute-done.18
  49.9 2.0 %collective-permute-start.19 = (f32[2,32,512]{2,1,0:T(8,128)S(1)}, f32[2,32,512]{2,1,0:T(8,128)S(1)}, u32[]{:S(2)}, u32[]{:S(2)}) collective-permute-start(f32[2,32,512]{2,1,0:T(8,128)S(1)} %maximum_bitcast_fusion.4), channel_id=1, source_target_pairs={{0,1},{1,0},{2,3},{3,2},{4,5},{5,4},{6,7},{7,6},{8,9},{9,8},{10,11... | collective-permute-start | bytes 393224 | tf_op jit(solution)/shard_map/ppermute | solution.py:32
  51.9 2.5 %collective-permute-start.11 = (f32[1,4,32,512]{3,2,1,0:T(8,128)S(1)}, f32[1,4,32,512]{3,2,1,0:T(8,128)S(1)}, u32[]{:S(2)}, u32[]{:S(2)}) collective-permute-start(f32[1,4,32,512]{3,2,1,0:T(8,128)S(1)} %bitcast.149), channel_id=1, source_target_pairs={{0,16},{8,24},{16,0},{24,8},{1,17},{9,25},{17,1},{25,9},{2,18},{10... | collective-permute-start | bytes 786440 | tf_op jit(solution)/shard_map/ppermute | solution.py:32
  54.5 0.0 collective-permute-done.15
  54.5 1.3 %collective-permute-start.16 = (f32[32,512]{1,0:T(8,128)S(1)}, f32[32,512]{1,0:T(8,128)S(1)}, u32[]{:S(2)}, u32[]{:S(2)}) collective-permute-start(f32[32,512]{1,0:T(8,128)S(1)} %add.35), channel_id=1, source_target_pairs={{0,4},{1,5},{2,6},{3,7},{4,0},{5,1},{6,2},{7,3},{8,12},{9,13},{10,... | collective-permute-start | bytes 196616 | tf_op jit(solution)/shard_map/ppermute | solution.py:32
  55.8 0.0 collective-permute-done.14
  55.8 0.0 collective-permute-done.19
  55.9 4.5 %collective-permute-done.16 = f32[32,512]{1,0:T(8,128)S(1)} collective-permute-done((f32[32,512]{1,0:T(8,128)S(1)}, f32[32,512]{1,0:T(8,128)S(1)}, u32[]{:S(2)}, u32[]{:S(2)}) %collective-permute-start.16) | collective-permute-done | bytes 65568 | tf_op jit(solution)/shard_map/ppermute | solution.py:32
  60.4 0.1 collective-permute-start.21
  60.5 0.1 pad_maximum_fusion.5
  60.6 2.0 %collective-permute-start.20 = (f32[5,32,512]{2,1,0:T(8,128)S(1)}, f32[5,32,512]{2,1,0:T(8,128)S(1)}, u32[]{:S(2)}, u32[]{:S(2)}) collective-permute-start(f32[5,32,512]{2,1,0:T(8,128)S(1)} %get-tuple-element.93), channel_id=1, source_target_pairs={{0,2},{1,3},{2,0},{3,1},{4,6},{5,7},{6,4},{7,5},{8,10},{9,11},{10,... | collective-permute-start | bytes 983048 | tf_op jit(solution)/shard_map/ppermute | solution.py:32
  62.5 1.6 %collective-permute-start.17 = (f32[5,32,512]{2,1,0:T(8,128)S(1)}, f32[5,32,512]{2,1,0:T(8,128)S(1)}, u32[]{:S(2)}, u32[]{:S(2)}) collective-permute-start(f32[5,32,512]{2,1,0:T(8,128)S(1)} %get-tuple-element.94), channel_id=1, source_target_pairs={{0,1},{1,0},{2,3},{3,2},{4,5},{5,4},{6,7},{7,6},{8,9},{9,8},{10,11... | collective-permute-start | bytes 983048 | tf_op jit(solution)/shard_map/ppermute | solution.py:32
  64.1 0.0 collective-permute-done.11
  64.2 0.1 collective-permute-start.12
  64.3 4.8 %collective-permute-done.20 = f32[5,32,512]{2,1,0:T(8,128)S(1)} collective-permute-done((f32[5,32,512]{2,1,0:T(8,128)S(1)}, f32[5,32,512]{2,1,0:T(8,128)S(1)}, u32[]{:S(2)}, u32[]{:S(2)}) %collective-permute-start.20) | collective-permute-done | bytes 327712 | tf_op jit(solution)/shard_map/ppermute | solution.py:32
  69.1 0.9 %collective-permute-done.17 = f32[5,32,512]{2,1,0:T(8,128)S(1)} collective-permute-done((f32[5,32,512]{2,1,0:T(8,128)S(1)}, f32[5,32,512]{2,1,0:T(8,128)S(1)}, u32[]{:S(2)}, u32[]{:S(2)}) %collective-permute-start.17) | collective-permute-done | bytes 327712 | tf_op jit(solution)/shard_map/ppermute | solution.py:32
  70.0 0.1 select_bitcast_fusion.3
  70.2 0.0 collective-permute-done.12
  70.2 0.1 select_bitcast_fusion.1
  70.3 0.0 copy-start.1
  70.3 0.1 pad_maximum_fusion
  70.4 0.4 shard_map.41
  70.9 0.0 collective-permute-done.21.refs_3_
  70.9 1.0 %copy-done.1 = f32[8,1,128,4,1,128]{5,4,3,2,1,0:T(1,128)S(1)} copy-done((f32[8,1,128,4,1,128]{5,4,3,2,1,0:T(1,128)S(1)}, f32[8,1,128,4,1,128]{5,4,3,2,1,0:T(1,128)}, u32[]{:S(2)}) %copy-start.1) | copy-done | bytes 2097176
  71.9 3.9 %shard_map.42 = f32[4096,128]{1,0:T(8,128)} custom-call(f32[4096,128]{1,0:T(8,128)S(1)} %bitcast.140, bf16[1024,256]{1,0:T(8,128)(2,1)S(1)} %get-tuple-element.49.urh_ref, bf16[1024,256]{1,0:T(8,128)(2,1)S(1)} %get-tuple-element.50.url_ref, bf16[256,512]{1,0:T(8,128)(2,1)S(1)} %get-tuple-element.57.uch_ref, bf16[256,512]{1,0:T(8,128)(2,1)S(1)} %get-tuple-element.58.ucl_ref, ...), custom_call_target="tpu_custom_call" | custom-call | flops 1610612736 | bytes 4194304 | tf_op jit(solution)/shard_map/pallas_call | solution.py:302
  (34 shorter events, 0.7 us)
Async XLA Ops:
  0.9 7.8 %collective-permute-start.1 = (f32[1,4,32,128]{3,2,1,0:T(8,128)S(1)}, f32[1,4,32,128]{3,2,1,0:T(8,128)S(1)}, u32[]{:S(2)}, u32[]{:S(2)}) collective-permute-start(f32[1,4,32,128]{3,2,1,0:T(8,128)S(1)} %get-tuple-element.91), channel_id=1, source_target_pairs={{0,4},{1,5},{2,6},{3,7},{4,0},{5,1},{6,2},{7,3},{8,12},{9,13},{10,... | collective-permute-start | bytes 196616 | tf_op jit(solution)/shard_map/ppermute | solution.py:32
  5.0 6.5 %collective-permute-start = (f32[1,4,32,128]{3,2,1,0:T(8,128)S(1)}, f32[1,4,32,128]{3,2,1,0:T(8,128)S(1)}, u32[]{:S(2)}, u32[]{:S(2)}) collective-permute-start(f32[1,4,32,128]{3,2,1,0:T(8,128)S(1)} %get-tuple-element.92), channel_id=1, source_target_pairs={{0,4},{1,5},{2,6},{3,7},{4,0},{5,1},{6,2},{7,3},{8,12},{9,13},{10,... | collective-permute-start | bytes 196616 | tf_op jit(solution)/shard_map/ppermute | solution.py:32
  5.1 1.6 %copy-start = (f32[8,1,128,4,1,128]{5,4,3,2,1,0:T(1,128)S(1)}, f32[8,1,128,4,1,128]{5,4,3,2,1,0:T(1,128)}, u32[]{:S(2)}) copy-start(f32[8,1,128,4,1,128]{5,4,3,2,1,0:T(1,128)} %param.3) | copy-start | bytes 6291460
  8.7 5.7 %collective-permute-start.2 = (f32[2,4,32,128]{3,2,1,0:T(8,128)S(1)}, f32[2,4,32,128]{3,2,1,0:T(8,128)S(1)}, u32[]{:S(2)}, u32[]{:S(2)}) collective-permute-start(f32[2,4,32,128]{3,2,1,0:T(8,128)S(1)} %maximum_bitcast_fusion.1), channel_id=1, source_target_pairs={{0,2},{1,3},{2,0},{3,1},{4,6},{5,7},{6,4},{7,5},{8,10},{9,11},{10,... | collective-permute-start | bytes 393224 | tf_op jit(solution)/shard_map/ppermute | solution.py:32
  11.5 5.4 %collective-permute-start.4 = (f32[2,4,32,128]{3,2,1,0:T(8,128)S(1)}, f32[2,4,32,128]{3,2,1,0:T(8,128)S(1)}, u32[]{:S(2)}, u32[]{:S(2)}) collective-permute-start(f32[2,4,32,128]{3,2,1,0:T(8,128)S(1)} %maximum_bitcast_fusion.2), channel_id=1, source_target_pairs={{0,1},{1,0},{2,3},{3,2},{4,5},{5,4},{6,7},{7,6},{8,9},{9,8},{10,11... | collective-permute-start | bytes 393224 | tf_op jit(solution)/shard_map/ppermute | solution.py:32
  14.4 7.9 %collective-permute-start.3 = (f32[4,4,32,128]{3,2,1,0:T(8,128)S(1)}, f32[4,4,32,128]{3,2,1,0:T(8,128)S(1)}, u32[]{:S(2)}, u32[]{:S(2)}) collective-permute-start(f32[4,4,32,128]{3,2,1,0:T(8,128)S(1)} %bitcast.150), channel_id=1, source_target_pairs={{0,1},{1,0},{2,3},{3,2},{4,5},{5,4},{6,7},{7,6},{8,9},{9,8},{10,11... | collective-permute-start | bytes 786440 | tf_op jit(solution)/shard_map/ppermute | solution.py:32
  17.0 7.0 %collective-permute-start.5 = (f32[4,4,32,128]{3,2,1,0:T(8,128)S(1)}, f32[4,4,32,128]{3,2,1,0:T(8,128)S(1)}, u32[]{:S(2)}, u32[]{:S(2)}) collective-permute-start(f32[4,4,32,128]{3,2,1,0:T(8,128)S(1)} %bitcast.151), channel_id=1, source_target_pairs={{0,2},{1,3},{2,0},{3,1},{4,6},{5,7},{6,4},{7,5},{8,10},{9,11},{10,... | collective-permute-start | bytes 786440 | tf_op jit(solution)/shard_map/ppermute | solution.py:32
  24.0 9.9 %copy-start.2 = (f32[256,256]{1,0:T(8,128)S(1)}, f32[256,256]{1,0:T(8,128)}, u32[]{:S(2)}) copy-start(f32[256,256]{1,0:T(8,128)} %t_ref.3) | copy-start | bytes 786436
  25.1 1.6 %collective-permute-start.6 = (f32[2,64,512]{2,1,0:T(8,128)S(1)}, f32[2,64,512]{2,1,0:T(8,128)S(1)}, u32[]{:S(2)}, u32[]{:S(2)}) collective-permute-start(f32[2,64,512]{2,1,0:T(8,128)S(1)} %get-tuple-element.43), channel_id=1, source_target_pairs={{0,8},{8,0},{16,24},{24,16},{1,9},{9,1},{17,25},{25,17},{2,10},{10... | collective-permute-start | bytes 786440 | tf_op jit(solution)/shard_map/ppermute | solution.py:32
  26.8 5.7 %collective-permute-start.7 = (f32[1,64,512]{2,1,0:T(8,128)S(1)}, f32[1,64,512]{2,1,0:T(8,128)S(1)}, u32[]{:S(2)}, u32[]{:S(2)}) collective-permute-start(f32[1,64,512]{2,1,0:T(8,128)S(1)} %constant_dynamic-slice_fusion), channel_id=1, source_target_pairs={{0,16},{8,24},{16,0},{24,8},{1,17},{9,25},{17,1},{25,9},{2,18},{10... | collective-permute-start | bytes 393224 | tf_op jit(solution)/shard_map/ppermute | solution.py:32
  32.5 2.4 %collective-permute-start.8 = (f32[64,512]{1,0:T(8,128)S(1)}, f32[64,512]{1,0:T(8,128)S(1)}, u32[]{:S(2)}, u32[]{:S(2)}) collective-permute-start(f32[64,512]{1,0:T(8,128)S(1)} %bitcast.152), channel_id=1, source_target_pairs={{0,0},{1,8},{2,16},{3,24},{4,4},{5,12},{6,20},{7,28},{8,1},{9,9},{... | collective-permute-start | bytes 393224 | tf_op jit(solution)/shard_map/ppermute | solution.py:202
  33.2 9.0 %collective-permute-start.9 = (f32[64,512]{1,0:T(8,128)S(1)}, f32[64,512]{1,0:T(8,128)S(1)}, u32[]{:S(2)}, u32[]{:S(2)}) collective-permute-start(f32[64,512]{1,0:T(8,128)S(1)} %copy_bitcast_fusion), channel_id=1, source_target_pairs={{0,0},{1,8},{2,16},{3,24},{4,4},{5,12},{6,20},{7,28},{8,1},{9,9},{... | collective-permute-start | bytes 393224 | tf_op jit(solution)/shard_map/ppermute | solution.py:202
  35.4 7.5 %collective-permute-start.10 = (f32[32,512]{1,0:T(8,128)S(1)}, f32[32,512]{1,0:T(8,128)S(1)}, u32[]{:S(2)}, u32[]{:S(2)}) collective-permute-start(f32[32,512]{1,0:T(8,128)S(1)} %shard_map.40), channel_id=1, source_target_pairs={{0,8},{8,0},{16,24},{24,16},{1,9},{9,1},{17,25},{25,17},{2,10},{10... | collective-permute-start | bytes 196616 | tf_op jit(solution)/shard_map/ppermute | solution.py:32
  39.8 9.8 %collective-permute-start.13 = (f32[1,32,512]{2,1,0:T(8,128)S(1)}, f32[1,32,512]{2,1,0:T(8,128)S(1)}, u32[]{:S(2)}, u32[]{:S(2)}) collective-permute-start(f32[1,32,512]{2,1,0:T(8,128)S(1)} %get-tuple-element.84), channel_id=1, source_target_pairs={{0,4},{1,5},{2,6},{3,7},{4,0},{5,1},{6,2},{7,3},{8,12},{9,13},{10,... | collective-permute-start | bytes 196616 | tf_op jit(solution)/shard_map/ppermute | solution.py:32
  42.3 7.6 %collective-permute-start.18 = (f32[1,32,512]{2,1,0:T(8,128)S(1)}, f32[1,32,512]{2,1,0:T(8,128)S(1)}, u32[]{:S(2)}, u32[]{:S(2)}) collective-permute-start(f32[1,32,512]{2,1,0:T(8,128)S(1)} %get-tuple-element.83), channel_id=1, source_target_pairs={{0,4},{1,5},{2,6},{3,7},{4,0},{5,1},{6,2},{7,3},{8,12},{9,13},{10,... | collective-permute-start | bytes 196616 | tf_op jit(solution)/shard_map/ppermute | solution.py:32
  42.9 11.6 %collective-permute-start.15 = (f32[32,512]{1,0:T(8,128)S(1)}, f32[32,512]{1,0:T(8,128)S(1)}, u32[]{:S(2)}, u32[]{:S(2)}) collective-permute-start(f32[32,512]{1,0:T(8,128)S(1)} %add.34), channel_id=1, source_target_pairs={{0,16},{8,24},{16,0},{24,8},{1,17},{9,25},{17,1},{25,9},{2,18},{10... | collective-permute-start | bytes 196616 | tf_op jit(solution)/shard_map/ppermute | solution.py:32
  49.6 6.1 %collective-permute-start.14 = (f32[2,32,512]{2,1,0:T(8,128)S(1)}, f32[2,32,512]{2,1,0:T(8,128)S(1)}, u32[]{:S(2)}, u32[]{:S(2)}) collective-permute-start(f32[2,32,512]{2,1,0:T(8,128)S(1)} %maximum_bitcast_fusion.3), channel_id=1, source_target_pairs={{0,2},{1,3},{2,0},{3,1},{4,6},{5,7},{6,4},{7,5},{8,10},{9,11},{10,... | collective-permute-start | bytes 393224 | tf_op jit(solution)/shard_map/ppermute | solution.py:32
  49.9 5.9 %collective-permute-start.19 = (f32[2,32,512]{2,1,0:T(8,128)S(1)}, f32[2,32,512]{2,1,0:T(8,128)S(1)}, u32[]{:S(2)}, u32[]{:S(2)}) collective-permute-start(f32[2,32,512]{2,1,0:T(8,128)S(1)} %maximum_bitcast_fusion.4), channel_id=1, source_target_pairs={{0,1},{1,0},{2,3},{3,2},{4,5},{5,4},{6,7},{7,6},{8,9},{9,8},{10,11... | collective-permute-start | bytes 393224 | tf_op jit(solution)/shard_map/ppermute | solution.py:32
  51.9 12.2 %collective-permute-start.11 = (f32[1,4,32,512]{3,2,1,0:T(8,128)S(1)}, f32[1,4,32,512]{3,2,1,0:T(8,128)S(1)}, u32[]{:S(2)}, u32[]{:S(2)}) collective-permute-start(f32[1,4,32,512]{3,2,1,0:T(8,128)S(1)} %bitcast.149), channel_id=1, source_target_pairs={{0,16},{8,24},{16,0},{24,8},{1,17},{9,25},{17,1},{25,9},{2,18},{10... | collective-permute-start | bytes 786440 | tf_op jit(solution)/shard_map/ppermute | solution.py:32
  54.5 5.9 %collective-permute-start.16 = (f32[32,512]{1,0:T(8,128)S(1)}, f32[32,512]{1,0:T(8,128)S(1)}, u32[]{:S(2)}, u32[]{:S(2)}) collective-permute-start(f32[32,512]{1,0:T(8,128)S(1)} %add.35), channel_id=1, source_target_pairs={{0,4},{1,5},{2,6},{3,7},{4,0},{5,1},{6,2},{7,3},{8,12},{9,13},{10,... | collective-permute-start | bytes 196616 | tf_op jit(solution)/shard_map/ppermute | solution.py:32
  60.4 10.5 %collective-permute-start.21 = (f32[1,32,512]{2,1,0:T(8,128)S(1)}, f32[1,32,512]{2,1,0:T(8,128)S(1)}, u32[]{:S(2)}, u32[]{:S(2)}) collective-permute-start(f32[1,32,512]{2,1,0:T(8,128)S(1)} %add_bitcast_fusion.refs_0_), channel_id=1, source_target_pairs={{0,3},{1,2},{2,1},{3,0},{4,7},{5,6},{6,5},{7,4},{8,11},{9,10},{10,... | collective-permute-start | bytes 196616 | tf_op jit(solution)/shard_map/ppermute | solution.py:32
  60.6 8.5 %collective-permute-start.20 = (f32[5,32,512]{2,1,0:T(8,128)S(1)}, f32[5,32,512]{2,1,0:T(8,128)S(1)}, u32[]{:S(2)}, u32[]{:S(2)}) collective-permute-start(f32[5,32,512]{2,1,0:T(8,128)S(1)} %get-tuple-element.93), channel_id=1, source_target_pairs={{0,2},{1,3},{2,0},{3,1},{4,6},{5,7},{6,4},{7,5},{8,10},{9,11},{10,... | collective-permute-start | bytes 983048 | tf_op jit(solution)/shard_map/ppermute | solution.py:32
  62.5 7.5 %collective-permute-start.17 = (f32[5,32,512]{2,1,0:T(8,128)S(1)}, f32[5,32,512]{2,1,0:T(8,128)S(1)}, u32[]{:S(2)}, u32[]{:S(2)}) collective-permute-start(f32[5,32,512]{2,1,0:T(8,128)S(1)} %get-tuple-element.94), channel_id=1, source_target_pairs={{0,1},{1,0},{2,3},{3,2},{4,5},{5,4},{6,7},{7,6},{8,9},{9,8},{10,11... | collective-permute-start | bytes 983048 | tf_op jit(solution)/shard_map/ppermute | solution.py:32
  64.2 6.0 %collective-permute-start.12 = (f32[2,4,32,512]{3,2,1,0:T(8,128)S(1)}, f32[2,4,32,512]{3,2,1,0:T(8,128)S(1)}, u32[]{:S(2)}, u32[]{:S(2)}) collective-permute-start(f32[2,4,32,512]{3,2,1,0:T(8,128)S(1)} %maximum_bitcast_fusion), channel_id=1, source_target_pairs={{0,8},{8,0},{16,24},{24,16},{1,9},{9,1},{17,25},{25,17},{2,10},{10... | collective-permute-start | bytes 1572872 | tf_op jit(solution)/shard_map/ppermute | solution.py:32
  70.3 1.6 %copy-start.1 = (f32[8,1,128,4,1,128]{5,4,3,2,1,0:T(1,128)S(1)}, f32[8,1,128,4,1,128]{5,4,3,2,1,0:T(1,128)}, u32[]{:S(2)}) copy-start(f32[8,1,128,4,1,128]{5,4,3,2,1,0:T(1,128)} %param.3) | copy-start | bytes 6291460
where the time goes:
time: 76.1 us; the launch traced here: 75.8 us
  starting transfers between devices  37.9 us (50%)
  waiting for transfers between devices  25.6 us (34%)
  Pallas kernels  7.35 us (10%)
  local copies, waits for them, and re-layouts  3.58 us (5%)
  other arithmetic  1.06 us (1%)
    ppermute x20, starting transfers between devices, swap(): return lax.ppermute(values, axis, [(i, i ^ mask) for i in range(n)])  36.5 us
    ppermute x20, waiting for transfers between devices, swap(): return lax.ppermute(values, axis, [(i, i ^ mask) for i in range(n)])  25.6 us
    pallas_call x1, Pallas kernels, per_device(): pl.pallas_call(functools.partial(update_kernel, orders, inner_upper), out...  3.91 us
    unnamed x6, local copies, waits for them, and re-layouts  2.64 us
  transfers between devices with their start and end apart: 22, of which 11 were waited for; matrix products, arithmetic and copies ran while one was open for 1% of the time, Pallas kernels for 3%

commit v1 on v0

--- a/solution.py
+++ b/solution.py
@@ -100,28 +100,40 @@
         inner_ref[:, side * nb : (side + 1) * nb] = inner[side * half : (side + 1) * half]
 
 
-def row_factor_kernel(t_ref, y_ref, high_ref, low_ref):
+def stack_left(values):
+    high, low = split(values)
+    return jnp.concatenate([high, high, low], axis=1)
+
+
+def stack_right(ref, values):
+    rows = values.shape[0]
+    high, low = split(values)
+    ref[:rows, :] = high
+    ref[rows : 2 * rows, :] = low
+    ref[2 * rows :, :] = high
+
+
+def row_factor_kernel(t_ref, y_ref, out_ref):
     row_tiles, nb, tile = y_ref.shape
     factor = split(t_ref[...])
     for a in range(row_tiles):
-        rows = slice(a * tile, (a + 1) * tile)
-        high_ref[rows, :], low_ref[rows, :] = split(dot3(factor, split(y_ref[a])).T)
-
-
-def column_factor_kernel(order, t_ref, cols_ref, high_ref, low_ref, z_ref, y):
+        out_ref[a * tile : (a + 1) * tile, :] = stack_left(dot3(factor, split(y_ref[a])).T)
+
+
+def column_factor_kernel(order, t_ref, cols_ref, out_ref, z_ref, y):
     slots, _, half, _ = cols_ref.shape
     for s in range(slots):
         for side in range(2):
             rows = slice((2 * s + side) * half, (2 * s + side + 1) * half)
             z_ref[rows, :] = cols_ref[slot(s, order), side]
             y[rows, :] = cols_ref[slot(s, order), 2 + side]
-    high_ref[...], low_ref[...] = split(dot3(split(t_ref[...]), split(y[...])))
+    stack_right(out_ref, dot3(split(t_ref[...]), split(y[...])))
 
 
 def update_kernel(
-    orders, inner_upper, a_ref, urh_ref, url_ref, uch_ref, ucl_ref, zc_ref, first_ref, second_ref, *refs
+    orders, inner_upper, a_ref, ur_ref, uc_ref, zc_ref, first_ref, second_ref, *refs
 ):
-    inners, (out_ref, inner, zt, block, result, read, write) = refs[:4], refs[4:]
+    inners, (out_ref, inner, w, zt, block, result, read, write) = refs[:4], refs[4:]
     near = lax.axis_index("pcol") & 3
     ratio, nb, cols = zt.shape
     nc, half = first_ref.shape[:2]
@@ -142,14 +154,13 @@
             for side in range(2):
                 at = pl.multiple_of((2 * (u * 4 + (near ^ r)) + side) * half, half)
                 inner[pl.ds(at, half), :] = inners[r][slot(u, inner_upper), :, side * nb : (side + 1) * nb]
-    uc = (uch_ref[...], ucl_ref[...])
-    w = split(zc_ref[...] - dot3(split(inner[...]), uc))
+    stack_right(w, zc_ref[...] - dot3(split(inner[...]), (uc_ref[:nb, :], uc_ref[nb : 2 * nb, :])))
     rows = lines // col_tiles
     count = rows // (ratio * tile)
     for i in range(chunks):
         at = slice(i * rows, (i + 1) * rows)
         turned = [zt[g, :, b * tile : (b + 1) * tile].T for b in range(i * count, (i + 1) * count) for g in range(ratio)]
-        total = dot3(split(jnp.concatenate(turned, axis=0)), uc) + dot3((urh_ref[at, :], url_ref[at, :]), w)
+        total = dot(stack_left(jnp.concatenate(turned, axis=0)), uc_ref[...]) + dot(ur_ref[at, :], w[...])
         reads[i].wait()
         for g in range(ratio * count):
             for b in range(col_tiles):
@@ -183,6 +194,7 @@
     group = pcol >> shift
     where = {
         "group": group,
+        "rounds": [(prow >> 1) ^ r for r in range(ny)],
         "share": (pcol & (np_ - 1)) * part,
         "col": {mask: (pcol & mask) != 0 for mask in masks},
         "row": {mask: (prow & mask) != 0 for mask in cols_order},
@@ -195,9 +207,9 @@
     def flat(p, q):
         return p * nc + q
 
-    def turn(values):
+    def turn(values, r):
         perm = [
-            (flat(p, g * np_ + s), flat(s, g * np_ + p)) for p in range(np_) for g in range(ratio) for s in range(np_)
+            (flat(p, g * np_ + s), flat(s, g * np_ + (p ^ r))) for p in range(np_) for g in range(ratio) for s in range(np_)
         ]
         return lax.ppermute(values, BOTH, perm)
 
@@ -234,24 +246,29 @@
         y_rows.reshape(col_tiles, ratio, nb, tile), (0, group, where["share"], 0), (col_tiles, 1, part, tile)
     )
     y_piece = jnp.transpose(y_piece.reshape(col_tiles, part, tile), (1, 0, 2)).reshape(part, cols)
+
+    turned = []
+    for r in range(ny):
+        message = lax.dynamic_index_in_dim(kept, where["rounds"][r], 0, keepdims=False)
+        turned.append(turn(message, 2 * r))
+    turned = sum(turned[1:], turned[0])
+    kept = lax.optimization_barrier(kept)
     for mask in cols_order[:-1]:
         low, high = where["half"][mask]
         pair = kept.reshape(2, mask // 2, part, cols)
         kept = lax.dynamic_index_in_dim(pair, low, 0, keepdims=False)
         kept = kept + swap(lax.dynamic_index_in_dim(pair, high, 0, keepdims=False), "prow", mask)
     piece = kept.reshape(part, cols)
-
-    turned = turn(piece)
-    y_cols = turn(y_piece).reshape(2, part // 2, cols)
-    urh, url = pl.pallas_call(
+    y_cols = turn(y_piece, 0).reshape(2, part // 2, cols)
+    u_rows = pl.pallas_call(
         row_factor_kernel,
-        out_shape=[shape(rows, nb, dtype=BF16)] * 2,
+        out_shape=shape(rows, 3 * nb, dtype=BF16),
         in_specs=[whole] * 2,
-        out_specs=[whole] * 2,
+        out_specs=whole,
         compiler_params=VMEM,
         cost_estimate=pl.CostEstimate(flops=6 * nb * nb * rows, bytes_accessed=rows * nb * 8, transcendentals=0),
     )(tfactor, y_rows)
-    turned, urh, url = lax.optimization_barrier((turned, urh, url))
+    turned, u_rows = lax.optimization_barrier((turned, u_rows))
     inner = pl.pallas_call(
         functools.partial(inner_kernel, shift),
         out_shape=shape(part // 2, 2 * nb),
@@ -262,7 +279,11 @@
     )(turned, y_rows)
     first, second = turned[None, : part // 2], turned[None, part // 2 :]
     first, second = lax.optimization_barrier(first), lax.optimization_barrier(second)
-    for mask in lead + rest[:-2]:
+    for mask in lead:
+        first = join(first, swap(first, "pcol", mask), col[mask])
+        came = swap(jnp.concatenate([second, inner[None]]), "pcol", mask)
+        second, inner = join(second, came[:-1], col[mask]), inner + came[-1]
+    for mask in rest[:-2]:
         first = join(first, swap(first, "pcol", mask), col[mask])
         second = join(second, swap(second, "pcol", mask), col[mask])
     first = join(first, swap(first, "pcol", far), col[far])
@@ -273,8 +294,6 @@
         inner = inner + swap(inner, "prow", mask)
         if mask == 1:
             columns, inner = lax.optimization_barrier((columns, inner))
-    for mask in lead:
-        inner = inner + swap(inner, "pcol", mask)
     inner = inner[None]
     for mask in rest[:-2]:
         inner = join(inner, swap(inner, "pcol", mask), col[mask])
@@ -286,11 +305,11 @@
     second = join(second, second_came[:blocks], col[far])
 
     columns = gather(columns, "prow", cols_order, row)
-    uch, ucl, zc = pl.pallas_call(
+    u_cols, zc = pl.pallas_call(
         functools.partial(column_factor_kernel, cols_order),
-        out_shape=[shape(nb, cols, dtype=BF16)] * 2 + [shape(nb, cols)],
+        out_shape=[shape(3 * nb, cols, dtype=BF16), shape(nb, cols)],
         in_specs=[whole] * 2,
-        out_specs=[whole] * 3,
+        out_specs=[whole] * 2,
         scratch_shapes=[pltpu.VMEM((nb, cols), F32)],
         compiler_params=VMEM,
         cost_estimate=pl.CostEstimate(flops=6 * nb * nb * cols, bytes_accessed=cols * nb * 8, transcendentals=0),
@@ -302,10 +321,11 @@
     result = pl.pallas_call(
         functools.partial(update_kernel, orders, inner_upper),
         out_shape=shape(rows * col_tiles, tile),
-        in_specs=[outside] + [whole] * 11,
+        in_specs=[outside] + [whole] * 9,
         out_specs=outside,
         scratch_shapes=[
             pltpu.VMEM((nb, nb), F32),
+            pltpu.VMEM((3 * nb, cols), BF16),
             pltpu.VMEM((ratio, nb, cols), F32),
             pltpu.VMEM((chunks, lines, tile), F32),
             pltpu.VMEM((chunks, lines, tile), F32),
@@ -314,7 +334,7 @@
         ],
         compiler_params=VMEM,
         cost_estimate=pl.CostEstimate(flops=12 * nb * rows * cols, bytes_accessed=rows * cols * 8, transcendentals=0),
-    )(block, urh, url, uch, ucl, zc, first, second, *near_inner)
+    )(block, u_rows, u_cols, zc, first, second, *near_inner)
     return result.reshape(trailing.shape)
 
 

time: 76.1 us -> 74 us (0.972)
  starting transfers between devices: 37.9 us -> 33.3 us
  waiting for transfers between devices: 25.6 us -> 28 us
    ppermute x20 -> x19, starting transfers between devices: 36.5 us -> 28.2 us  [swap(): return lax.ppermute(values, axis, [(i, i ^ mask) for i in range(n)])]
    ppermute x2 -> x3, starting transfers between devices: 1.34 us -> 5.15 us  [turn(): return lax.ppermute(values, BOTH, perm)]
    ppermute x20 -> x19, waiting for transfers between devices: 25.6 us -> 28 us  [swap(): return lax.ppermute(values, axis, [(i, i ^ mask) for i in range(n)])]
  transfers between devices with their start and end apart: 22 -> 22, of which waited for: 11 -> 15; matrix products, arithmetic and copies ran while one was open for 1% -> 2% of each run, Pallas kernels for 3% -> 3%
where the time goes in v1:
time: 74 us; the launch traced here: 73.7 us
  starting transfers between devices  33.3 us (45%)
  waiting for transfers between devices  28 us (38%)
  Pallas kernels  7.26 us (10%)
  local copies, waits for them, and re-layouts  3.61 us (5%)
  other arithmetic  1.09 us (1%)
    ppermute x19, starting transfers between devices, swap(): return lax.ppermute(values, axis, [(i, i ^ mask) for i in range(n)])  28.2 us
    ppermute x19, waiting for transfers between devices, swap(): return lax.ppermute(values, axis, [(i, i ^ mask) for i in range(n)])  28 us
    ppermute x3, starting transfers between devices, turn(): return lax.ppermute(values, BOTH, perm)  5.15 us
    pallas_call x1, Pallas kernels, per_device(): pl.pallas_call(functools.partial(update_kernel, orders, inner_upper), out...  3.83 us
    unnamed x6, local copies, waits for them, and re-layouts  2.64 us
  transfers between devices with their start and end apart: 22, of which 15 were waited for; matrix products, arithmetic and copies ran while one was open for 2% of the time, Pallas kernels for 3%

profile of v1, /device:TPU:0, one launch (start us, length us, event | category | flops | bytes accessed | tf_op | source)
XLA Modules:
  0.0 73.7 jit_solution(14108899380671504229)
XLA Ops:
  0.0 0.9 %slice_bitcast_fusion.3 = (f32[1,4,32,128]{3,2,1,0:T(8,128)S(1)}, f32[1,4,32,128]{3,2,1,0:T(8,128)S(1)}) fusion(f32[8,32,128]{2,1,0:T(8,128)} %bitcast.162), kind=kLoop, calls=%fused_computation.56 | loop fusion | bytes 262144 | tf_op jit(solution)/shard_map/broadcast_in_dim | solution.py:227
  0.9 4.1 %collective-permute-start.1 = (f32[1,4,32,128]{3,2,1,0:T(8,128)S(1)}, f32[1,4,32,128]{3,2,1,0:T(8,128)S(1)}, u32[]{:S(2)}, u32[]{:S(2)}) collective-permute-start(f32[1,4,32,128]{3,2,1,0:T(8,128)S(1)} %get-tuple-element.89), channel_id=1, source_target_pairs={{0,4},{1,5},{2,6},{3,7},{4,0},{5,1},{6,2},{7,3},{8,12},{9,13},{10,... | collective-permute-start | bytes 196616 | tf_op jit(solution)/shard_map/ppermute | solution.py:32
  5.0 0.1 collective-permute-start
  5.1 0.0 copy-start
  5.1 1.6 %copy-done = f32[8,1,128,4,1,128]{5,4,3,2,1,0:T(1,128)S(1)} copy-done((f32[8,1,128,4,1,128]{5,4,3,2,1,0:T(1,128)S(1)}, f32[8,1,128,4,1,128]{5,4,3,2,1,0:T(1,128)}, u32[]{:S(2)}) %copy-start) | copy-done | bytes 2097176
  6.7 0.5 shard_map.37
  7.2 1.5 %collective-permute-done.1 = f32[1,4,32,128]{3,2,1,0:T(8,128)S(1)} collective-permute-done((f32[1,4,32,128]{3,2,1,0:T(8,128)S(1)}, f32[1,4,32,128]{3,2,1,0:T(8,128)S(1)}, u32[]{:S(2)}, u32[]{:S(2)}) %collective-permute-start.1) | collective-permute-done | bytes 65568 | tf_op jit(solution)/shard_map/ppermute | solution.py:32
  8.7 2.1 %collective-permute-start.2 = (f32[2,4,32,128]{3,2,1,0:T(8,128)S(1)}, f32[2,4,32,128]{3,2,1,0:T(8,128)S(1)}, u32[]{:S(2)}, u32[]{:S(2)}) collective-permute-start(f32[2,4,32,128]{3,2,1,0:T(8,128)S(1)} %maximum_bitcast_fusion.1), channel_id=1, source_target_pairs={{0,2},{1,3},{2,0},{3,1},{4,6},{5,7},{6,4},{7,5},{8,10},{9,11},{10,... | collective-permute-start | bytes 393224 | tf_op jit(solution)/shard_map/ppermute | solution.py:32
  10.8 0.6 collective-permute-done
  11.5 1.8 %collective-permute-start.4 = (f32[2,4,32,128]{3,2,1,0:T(8,128)S(1)}, f32[2,4,32,128]{3,2,1,0:T(8,128)S(1)}, u32[]{:S(2)}, u32[]{:S(2)}) collective-permute-start(f32[2,4,32,128]{3,2,1,0:T(8,128)S(1)} %maximum_bitcast_fusion.2), channel_id=1, source_target_pairs={{0,1},{1,0},{2,3},{3,2},{4,5},{5,4},{6,7},{7,6},{8,9},{9,8},{10,11... | collective-permute-start | bytes 393224 | tf_op jit(solution)/shard_map/ppermute | solution.py:32
  13.2 1.1 %collective-permute-done.2 = f32[2,4,32,128]{3,2,1,0:T(8,128)S(1)} collective-permute-done((f32[2,4,32,128]{3,2,1,0:T(8,128)S(1)}, f32[2,4,32,128]{3,2,1,0:T(8,128)S(1)}, u32[]{:S(2)}, u32[]{:S(2)}) %collective-permute-start.2) | collective-permute-done | bytes 131104 | tf_op jit(solution)/shard_map/ppermute | solution.py:32
  14.4 1.6 %collective-permute-start.3 = (f32[4,4,32,128]{3,2,1,0:T(8,128)S(1)}, f32[4,4,32,128]{3,2,1,0:T(8,128)S(1)}, u32[]{:S(2)}, u32[]{:S(2)}) collective-permute-start(f32[4,4,32,128]{3,2,1,0:T(8,128)S(1)} %bitcast.159), channel_id=1, source_target_pairs={{0,1},{1,0},{2,3},{3,2},{4,5},{5,4},{6,7},{7,6},{8,9},{9,8},{10,11... | collective-permute-start | bytes 786440 | tf_op jit(solution)/shard_map/ppermute | solution.py:32
  16.1 0.8 %collective-permute-done.4 = f32[2,4,32,128]{3,2,1,0:T(8,128)S(1)} collective-permute-done((f32[2,4,32,128]{3,2,1,0:T(8,128)S(1)}, f32[2,4,32,128]{3,2,1,0:T(8,128)S(1)}, u32[]{:S(2)}, u32[]{:S(2)}) %collective-permute-start.4) | collective-permute-done | bytes 131104 | tf_op jit(solution)/shard_map/ppermute | solution.py:32
  17.0 0.9 %collective-permute-start.5 = (f32[4,4,32,128]{3,2,1,0:T(8,128)S(1)}, f32[4,4,32,128]{3,2,1,0:T(8,128)S(1)}, u32[]{:S(2)}, u32[]{:S(2)}) collective-permute-start(f32[4,4,32,128]{3,2,1,0:T(8,128)S(1)} %bitcast.160), channel_id=1, source_target_pairs={{0,2},{1,3},{2,0},{3,1},{4,6},{5,7},{6,4},{7,5},{8,10},{9,11},{10,... | collective-permute-start | bytes 786440 | tf_op jit(solution)/shard_map/ppermute | solution.py:32
  17.9 4.5 %collective-permute-done.3 = f32[4,4,32,128]{3,2,1,0:T(8,128)S(1)} collective-permute-done((f32[4,4,32,128]{3,2,1,0:T(8,128)S(1)}, f32[4,4,32,128]{3,2,1,0:T(8,128)S(1)}, u32[]{:S(2)}, u32[]{:S(2)}) %collective-permute-start.3) | collective-permute-done | bytes 262176 | tf_op jit(solution)/shard_map/ppermute | solution.py:32
  22.3 0.1 select_bitcast_fusion.11
  22.4 1.5 %collective-permute-done.5 = f32[4,4,32,128]{3,2,1,0:T(8,128)S(1)} collective-permute-done((f32[4,4,32,128]{3,2,1,0:T(8,128)S(1)}, f32[4,4,32,128]{3,2,1,0:T(8,128)S(1)}, u32[]{:S(2)}, u32[]{:S(2)}) %collective-permute-start.5) | collective-permute-done | bytes 262176 | tf_op jit(solution)/shard_map/ppermute | solution.py:32
  24.0 0.0 copy-start.2
  24.0 1.1 %shard_map.38 = (f32[8,256,128]{2,1,0:T(8,128)S(1)}, f32[2,64,512]{2,1,0:T(8,128)S(1)}, f32[2,64,512]{2,1,0:T(8,128)S(1)}) custom-call(bf16[1024,512]{1,0:T(8,128)(2,1)S(1)} %get-tuple-element.34.ah_ref, bf16[1024,512]{1,0:T(8,128)(2,1)S(1)} %get-tuple-element.35.al_ref, f32[8,4,32,128]{3,2,1,0:T(8,128)S(1)} %bitcast.153, f32[8,4,32,128]{3,2,1,0:T(8,128)S(1)} %bitcast.154), custom_call_target="tpu_custom_call" | custom-call | flops 805306368 | bytes 4194304 | tf_op jit(solution)/shard_map/pallas_call | solution.py:234
  25.1 0.1 collective-permute-start.6
  25.2 0.7 collective-permute-start.10
  25.9 0.8 %collective-permute-done.6 = f32[2,64,512]{2,1,0:T(8,128)S(1)} collective-permute-done((f32[2,64,512]{2,1,0:T(8,128)S(1)}, f32[2,64,512]{2,1,0:T(8,128)S(1)}, u32[]{:S(2)}, u32[]{:S(2)}) %collective-permute-start.6) | collective-permute-done | bytes 262176 | tf_op jit(solution)/shard_map/ppermute | solution.py:32
  26.8 3.8 %collective-permute-start.8 = (f32[64,512]{1,0:T(8,128)S(1)}, f32[64,512]{1,0:T(8,128)S(1)}, u32[]{:S(2)}, u32[]{:S(2)}) collective-permute-start(f32[64,512]{1,0:T(8,128)S(1)} %get-tuple-element.73), channel_id=1, source_target_pairs={{0,2},{1,10},{2,18},{3,26},{4,6},{5,14},{6,22},{7,30},{8,3},{9,11}... | collective-permute-start | bytes 393224 | tf_op jit(solution)/shard_map/ppermute | solution.py:214
  30.6 0.7 collective-permute-start.7
  31.3 0.0 copy-done.2
  31.3 1.0 %shard_map.39.ur_ref = bf16[1024,768]{1,0:T(8,128)(2,1)S(1)} custom-call(f32[256,256]{1,0:T(8,128)S(1)} %copy-done.2, f32[8,256,128]{2,1,0:T(8,128)S(1)} %get-tuple-element.44.y_ref), custom_call_target="tpu_custom_call" | custom-call | flops 402653184 | bytes 2097152 | tf_op jit(solution)/shard_map/pallas_call | solution.py:263
  32.4 2.8 %collective-permute-start.9 = (f32[1,64,512]{2,1,0:T(8,128)S(1)}, f32[1,64,512]{2,1,0:T(8,128)S(1)}, u32[]{:S(2)}, u32[]{:S(2)}) collective-permute-start(f32[1,64,512]{2,1,0:T(8,128)S(1)} %constant_dynamic-slice_fusion), channel_id=1, source_target_pairs={{0,16},{8,24},{16,0},{24,8},{1,17},{9,25},{17,1},{25,9},{2,18},{10... | collective-permute-start | bytes 393224 | tf_op jit(solution)/shard_map/ppermute | solution.py:32
  35.2 0.0 collective-permute-done.8
  35.2 0.0 collective-permute-done.7
  35.2 2.6 %collective-permute-start.15 = (f32[1,32,512]{2,1,0:T(8,128)S(1)}, f32[1,32,512]{2,1,0:T(8,128)S(1)}, u32[]{:S(2)}, u32[]{:S(2)}) collective-permute-start(f32[1,32,512]{2,1,0:T(8,128)S(1)} %get-tuple-element.83), channel_id=1, source_target_pairs={{0,4},{1,5},{2,6},{3,7},{4,0},{5,1},{6,2},{7,3},{8,12},{9,13},{10,... | collective-permute-start | bytes 196616 | tf_op jit(solution)/shard_map/ppermute | solution.py:32
  37.8 0.4 shard_map.40
  38.2 0.4 collective-permute-start.11
  38.7 1.2 %collective-permute-done.9 = f32[1,64,512]{2,1,0:T(8,128)S(1)} collective-permute-done((f32[1,64,512]{2,1,0:T(8,128)S(1)}, f32[1,64,512]{2,1,0:T(8,128)S(1)}, u32[]{:S(2)}, u32[]{:S(2)}) %collective-permute-start.9) | collective-permute-done | bytes 131104 | tf_op jit(solution)/shard_map/ppermute | solution.py:32
  39.9 0.0 collective-permute-done.10
  39.9 0.5 collective-permute-done.15
  40.5 4.7 %collective-permute-start.16 = (f32[2,32,512]{2,1,0:T(8,128)S(1)}, f32[2,32,512]{2,1,0:T(8,128)S(1)}, u32[]{:S(2)}, u32[]{:S(2)}) collective-permute-start(f32[2,32,512]{2,1,0:T(8,128)S(1)} %maximum_bitcast_fusion.3), channel_id=1, source_target_pairs={{0,2},{1,3},{2,0},{3,1},{4,6},{5,7},{6,4},{7,5},{8,10},{9,11},{10,... | collective-permute-start | bytes 393224 | tf_op jit(solution)/shard_map/ppermute | solution.py:32
  45.2 4.5 %collective-permute-done.11 = f32[2,32,512]{2,1,0:T(8,128)S(1)} collective-permute-done((f32[2,32,512]{2,1,0:T(8,128)S(1)}, f32[2,32,512]{2,1,0:T(8,128)S(1)}, u32[]{:S(2)}, u32[]{:S(2)}) %collective-permute-start.11) | collective-permute-done | bytes 131104 | tf_op jit(solution)/shard_map/ppermute | solution.py:32
  49.7 0.7 collective-permute-start.12
  50.4 0.4 collective-permute-start.19
  50.9 0.4 collective-permute-done.12
  51.3 1.9 %collective-permute-start.17 = (f32[32,512]{1,0:T(8,128)S(1)}, f32[32,512]{1,0:T(8,128)S(1)}, u32[]{:S(2)}, u32[]{:S(2)}) collective-permute-start(f32[32,512]{1,0:T(8,128)S(1)} %add.48), channel_id=1, source_target_pairs={{0,16},{8,24},{16,0},{24,8},{1,17},{9,25},{17,1},{25,9},{2,18},{10... | collective-permute-start | bytes 196616 | tf_op jit(solution)/shard_map/ppermute | solution.py:32
  53.2 0.2 collective-permute-start.13
  53.4 0.0 collective-permute-done.16
  53.4 2.5 %collective-permute-done.19 = f32[2,32,512]{2,1,0:T(8,128)S(1)} collective-permute-done((f32[2,32,512]{2,1,0:T(8,128)S(1)}, f32[2,32,512]{2,1,0:T(8,128)S(1)}, u32[]{:S(2)}, u32[]{:S(2)}) %collective-permute-start.19) | collective-permute-done | bytes 131104 | tf_op jit(solution)/shard_map/ppermute | solution.py:32
  56.0 0.0 collective-permute-done.17
  56.0 1.0 %collective-permute-start.21 = (f32[1,32,512]{2,1,0:T(8,128)S(1)}, f32[1,32,512]{2,1,0:T(8,128)S(1)}, u32[]{:S(2)}, u32[]{:S(2)}) collective-permute-start(f32[1,32,512]{2,1,0:T(8,128)S(1)} %add_bitcast_fusion.refs_0_), channel_id=1, source_target_pairs={{0,3},{1,2},{2,1},{3,0},{4,7},{5,6},{6,5},{7,4},{8,11},{9,10},{10,... | collective-permute-start | bytes 196616 | tf_op jit(solution)/shard_map/ppermute | solution.py:32
  57.0 0.1 pad_maximum_fusion.5
  57.0 1.8 %collective-permute-start.20 = (f32[5,32,512]{2,1,0:T(8,128)S(1)}, f32[5,32,512]{2,1,0:T(8,128)S(1)}, u32[]{:S(2)}, u32[]{:S(2)}) collective-permute-start(f32[5,32,512]{2,1,0:T(8,128)S(1)} %get-tuple-element.91), channel_id=1, source_target_pairs={{0,2},{1,3},{2,0},{3,1},{4,6},{5,7},{6,4},{7,5},{8,10},{9,11},{10,... | collective-permute-start | bytes 983048 | tf_op jit(solution)/shard_map/ppermute | solution.py:32
  58.8 0.8 %collective-permute-start.18 = (f32[5,32,512]{2,1,0:T(8,128)S(1)}, f32[5,32,512]{2,1,0:T(8,128)S(1)}, u32[]{:S(2)}, u32[]{:S(2)}) collective-permute-start(f32[5,32,512]{2,1,0:T(8,128)S(1)} %get-tuple-element.92), channel_id=1, source_target_pairs={{0,1},{1,0},{2,3},{3,2},{4,5},{5,4},{6,7},{7,6},{8,9},{9,8},{10,11... | collective-permute-start | bytes 983048 | tf_op jit(solution)/shard_map/ppermute | solution.py:32
  59.7 1.7 %collective-permute-done.13 = f32[1,4,32,512]{3,2,1,0:T(8,128)S(1)} collective-permute-done((f32[1,4,32,512]{3,2,1,0:T(8,128)S(1)}, f32[1,4,32,512]{3,2,1,0:T(8,128)S(1)}, u32[]{:S(2)}, u32[]{:S(2)}) %collective-permute-start.13) | collective-permute-done | bytes 262176 | tf_op jit(solution)/shard_map/ppermute | solution.py:32
  61.4 0.1 collective-permute-start.14
  61.5 5.6 %collective-permute-done.20 = f32[5,32,512]{2,1,0:T(8,128)S(1)} collective-permute-done((f32[5,32,512]{2,1,0:T(8,128)S(1)}, f32[5,32,512]{2,1,0:T(8,128)S(1)}, u32[]{:S(2)}, u32[]{:S(2)}) %collective-permute-start.20) | collective-permute-done | bytes 327712 | tf_op jit(solution)/shard_map/ppermute | solution.py:32
  67.1 0.9 %collective-permute-done.18 = f32[5,32,512]{2,1,0:T(8,128)S(1)} collective-permute-done((f32[5,32,512]{2,1,0:T(8,128)S(1)}, f32[5,32,512]{2,1,0:T(8,128)S(1)}, u32[]{:S(2)}, u32[]{:S(2)}) %collective-permute-start.18) | collective-permute-done | bytes 327712 | tf_op jit(solution)/shard_map/ppermute | solution.py:32
  68.0 0.1 select_bitcast_fusion.3
  68.2 0.0 collective-permute-done.14
  68.2 0.1 select_bitcast_fusion.1
  68.3 0.0 copy-start.1
  68.3 0.1 pad_maximum_fusion
  68.4 0.4 shard_map.41
  68.9 0.0 collective-permute-done.21.refs_3_
  68.9 1.0 %copy-done.1 = f32[8,1,128,4,1,128]{5,4,3,2,1,0:T(1,128)S(1)} copy-done((f32[8,1,128,4,1,128]{5,4,3,2,1,0:T(1,128)S(1)}, f32[8,1,128,4,1,128]{5,4,3,2,1,0:T(1,128)}, u32[]{:S(2)}) %copy-start.1) | copy-done | bytes 2097176
  69.9 3.8 %shard_map.42 = f32[4096,128]{1,0:T(8,128)} custom-call(f32[4096,128]{1,0:T(8,128)S(1)} %bitcast.148, bf16[1024,768]{1,0:T(8,128)(2,1)S(1)} %shard_map.39.ur_ref, bf16[768,512]{1,0:T(8,128)(2,1)S(1)} %get-tuple-element.54.uc_ref, f32[256,512]{1,0:T(8,128)S(1)} %get-tuple-element.55.zc_ref, f32[8,32,512]{2,1,0:T(8,128)S(1)} %bitcast.152, ...), custom_call_target="tpu_custom_call" | custom-call | flops 1610612736 | bytes 4194304 | tf_op jit(solution)/shard_map/pallas_call | solution.py:321
  (37 shorter events, 0.7 us)
Async XLA Ops:
  0.9 7.8 %collective-permute-start.1 = (f32[1,4,32,128]{3,2,1,0:T(8,128)S(1)}, f32[1,4,32,128]{3,2,1,0:T(8,128)S(1)}, u32[]{:S(2)}, u32[]{:S(2)}) collective-permute-start(f32[1,4,32,128]{3,2,1,0:T(8,128)S(1)} %get-tuple-element.89), channel_id=1, source_target_pairs={{0,4},{1,5},{2,6},{3,7},{4,0},{5,1},{6,2},{7,3},{8,12},{9,13},{10,... | collective-permute-start | bytes 196616 | tf_op jit(solution)/shard_map/ppermute | solution.py:32
  5.0 6.5 %collective-permute-start = (f32[1,4,32,128]{3,2,1,0:T(8,128)S(1)}, f32[1,4,32,128]{3,2,1,0:T(8,128)S(1)}, u32[]{:S(2)}, u32[]{:S(2)}) collective-permute-start(f32[1,4,32,128]{3,2,1,0:T(8,128)S(1)} %get-tuple-element.90), channel_id=1, source_target_pairs={{0,4},{1,5},{2,6},{3,7},{4,0},{5,1},{6,2},{7,3},{8,12},{9,13},{10,... | collective-permute-start | bytes 196616 | tf_op jit(solution)/shard_map/ppermute | solution.py:32
  5.1 1.6 %copy-start = (f32[8,1,128,4,1,128]{5,4,3,2,1,0:T(1,128)S(1)}, f32[8,1,128,4,1,128]{5,4,3,2,1,0:T(1,128)}, u32[]{:S(2)}) copy-start(f32[8,1,128,4,1,128]{5,4,3,2,1,0:T(1,128)} %param.3) | copy-start | bytes 6291460
  8.7 5.7 %collective-permute-start.2 = (f32[2,4,32,128]{3,2,1,0:T(8,128)S(1)}, f32[2,4,32,128]{3,2,1,0:T(8,128)S(1)}, u32[]{:S(2)}, u32[]{:S(2)}) collective-permute-start(f32[2,4,32,128]{3,2,1,0:T(8,128)S(1)} %maximum_bitcast_fusion.1), channel_id=1, source_target_pairs={{0,2},{1,3},{2,0},{3,1},{4,6},{5,7},{6,4},{7,5},{8,10},{9,11},{10,... | collective-permute-start | bytes 393224 | tf_op jit(solution)/shard_map/ppermute | solution.py:32
  11.5 5.4 %collective-permute-start.4 = (f32[2,4,32,128]{3,2,1,0:T(8,128)S(1)}, f32[2,4,32,128]{3,2,1,0:T(8,128)S(1)}, u32[]{:S(2)}, u32[]{:S(2)}) collective-permute-start(f32[2,4,32,128]{3,2,1,0:T(8,128)S(1)} %maximum_bitcast_fusion.2), channel_id=1, source_target_pairs={{0,1},{1,0},{2,3},{3,2},{4,5},{5,4},{6,7},{7,6},{8,9},{9,8},{10,11... | collective-permute-start | bytes 393224 | tf_op jit(solution)/shard_map/ppermute | solution.py:32
  14.4 7.9 %collective-permute-start.3 = (f32[4,4,32,128]{3,2,1,0:T(8,128)S(1)}, f32[4,4,32,128]{3,2,1,0:T(8,128)S(1)}, u32[]{:S(2)}, u32[]{:S(2)}) collective-permute-start(f32[4,4,32,128]{3,2,1,0:T(8,128)S(1)} %bitcast.159), channel_id=1, source_target_pairs={{0,1},{1,0},{2,3},{3,2},{4,5},{5,4},{6,7},{7,6},{8,9},{9,8},{10,11... | collective-permute-start | bytes 786440 | tf_op jit(solution)/shard_map/ppermute | solution.py:32
  17.0 7.0 %collective-permute-start.5 = (f32[4,4,32,128]{3,2,1,0:T(8,128)S(1)}, f32[4,4,32,128]{3,2,1,0:T(8,128)S(1)}, u32[]{:S(2)}, u32[]{:S(2)}) collective-permute-start(f32[4,4,32,128]{3,2,1,0:T(8,128)S(1)} %bitcast.160), channel_id=1, source_target_pairs={{0,2},{1,3},{2,0},{3,1},{4,6},{5,7},{6,4},{7,5},{8,10},{9,11},{10,... | collective-permute-start | bytes 786440 | tf_op jit(solution)/shard_map/ppermute | solution.py:32
  24.0 7.2 %copy-start.2 = (f32[256,256]{1,0:T(8,128)S(1)}, f32[256,256]{1,0:T(8,128)}, u32[]{:S(2)}) copy-start(f32[256,256]{1,0:T(8,128)} %t_ref.3) | copy-start | bytes 786436
  25.1 1.6 %collective-permute-start.6 = (f32[2,64,512]{2,1,0:T(8,128)S(1)}, f32[2,64,512]{2,1,0:T(8,128)S(1)}, u32[]{:S(2)}, u32[]{:S(2)}) collective-permute-start(f32[2,64,512]{2,1,0:T(8,128)S(1)} %get-tuple-element.41), channel_id=1, source_target_pairs={{0,8},{8,0},{16,24},{24,16},{1,9},{9,1},{17,25},{25,17},{2,10},{10... | collective-permute-start | bytes 786440 | tf_op jit(solution)/shard_map/ppermute | solution.py:32
  25.2 14.7 %collective-permute-start.10 = (f32[64,512]{1,0:T(8,128)S(1)}, f32[64,512]{1,0:T(8,128)S(1)}, u32[]{:S(2)}, u32[]{:S(2)}) collective-permute-start(f32[64,512]{1,0:T(8,128)S(1)} %copy_bitcast_fusion), channel_id=1, source_target_pairs={{0,0},{1,8},{2,16},{3,24},{4,4},{5,12},{6,20},{7,28},{8,1},{9,9},{... | collective-permute-start | bytes 393224 | tf_op jit(solution)/shard_map/ppermute | solution.py:214
  26.8 8.4 %collective-permute-start.8 = (f32[64,512]{1,0:T(8,128)S(1)}, f32[64,512]{1,0:T(8,128)S(1)}, u32[]{:S(2)}, u32[]{:S(2)}) collective-permute-start(f32[64,512]{1,0:T(8,128)S(1)} %get-tuple-element.73), channel_id=1, source_target_pairs={{0,2},{1,10},{2,18},{3,26},{4,6},{5,14},{6,22},{7,30},{8,3},{9,11}... | collective-permute-start | bytes 393224 | tf_op jit(solution)/shard_map/ppermute | solution.py:214
  30.6 4.6 %collective-permute-start.7 = (f32[64,512]{1,0:T(8,128)S(1)}, f32[64,512]{1,0:T(8,128)S(1)}, u32[]{:S(2)}, u32[]{:S(2)}) collective-permute-start(f32[64,512]{1,0:T(8,128)S(1)} %get-tuple-element.74), channel_id=1, source_target_pairs={{0,0},{1,8},{2,16},{3,24},{4,4},{5,12},{6,20},{7,28},{8,1},{9,9},{... | collective-permute-start | bytes 393224 | tf_op jit(solution)/shard_map/ppermute | solution.py:214
  32.4 7.5 %collective-permute-start.9 = (f32[1,64,512]{2,1,0:T(8,128)S(1)}, f32[1,64,512]{2,1,0:T(8,128)S(1)}, u32[]{:S(2)}, u32[]{:S(2)}) collective-permute-start(f32[1,64,512]{2,1,0:T(8,128)S(1)} %constant_dynamic-slice_fusion), channel_id=1, source_target_pairs={{0,16},{8,24},{16,0},{24,8},{1,17},{9,25},{17,1},{25,9},{2,18},{10... | collective-permute-start | bytes 393224 | tf_op jit(solution)/shard_map/ppermute | solution.py:32
  35.2 5.2 %collective-permute-start.15 = (f32[1,32,512]{2,1,0:T(8,128)S(1)}, f32[1,32,512]{2,1,0:T(8,128)S(1)}, u32[]{:S(2)}, u32[]{:S(2)}) collective-permute-start(f32[1,32,512]{2,1,0:T(8,128)S(1)} %get-tuple-element.83), channel_id=1, source_target_pairs={{0,4},{1,5},{2,6},{3,7},{4,0},{5,1},{6,2},{7,3},{8,12},{9,13},{10,... | collective-permute-start | bytes 196616 | tf_op jit(solution)/shard_map/ppermute | solution.py:32
  38.2 11.4 %collective-permute-start.11 = (f32[2,32,512]{2,1,0:T(8,128)S(1)}, f32[2,32,512]{2,1,0:T(8,128)S(1)}, u32[]{:S(2)}, u32[]{:S(2)}) collective-permute-start(f32[2,32,512]{2,1,0:T(8,128)S(1)} %pad_maximum_fusion.12), channel_id=1, source_target_pairs={{0,4},{1,5},{2,6},{3,7},{4,0},{5,1},{6,2},{7,3},{8,12},{9,13},{10,... | collective-permute-start | bytes 393224 | tf_op jit(solution)/shard_map/ppermute | solution.py:32
  40.5 12.9 %collective-permute-start.16 = (f32[2,32,512]{2,1,0:T(8,128)S(1)}, f32[2,32,512]{2,1,0:T(8,128)S(1)}, u32[]{:S(2)}, u32[]{:S(2)}) collective-permute-start(f32[2,32,512]{2,1,0:T(8,128)S(1)} %maximum_bitcast_fusion.3), channel_id=1, source_target_pairs={{0,2},{1,3},{2,0},{3,1},{4,6},{5,7},{6,4},{7,5},{8,10},{9,11},{10,... | collective-permute-start | bytes 393224 | tf_op jit(solution)/shard_map/ppermute | solution.py:32
  49.7 1.6 %collective-permute-start.12 = (f32[32,512]{1,0:T(8,128)S(1)}, f32[32,512]{1,0:T(8,128)S(1)}, u32[]{:S(2)}, u32[]{:S(2)}) collective-permute-start(f32[32,512]{1,0:T(8,128)S(1)} %fusion), channel_id=1, source_target_pairs={{0,8},{8,0},{16,24},{24,16},{1,9},{9,1},{17,25},{25,17},{2,10},{10... | collective-permute-start | bytes 196616 | tf_op jit(solution)/shard_map/ppermute | solution.py:32
  50.4 5.5 %collective-permute-start.19 = (f32[2,32,512]{2,1,0:T(8,128)S(1)}, f32[2,32,512]{2,1,0:T(8,128)S(1)}, u32[]{:S(2)}, u32[]{:S(2)}) collective-permute-start(f32[2,32,512]{2,1,0:T(8,128)S(1)} %maximum_bitcast_fusion.4), channel_id=1, source_target_pairs={{0,1},{1,0},{2,3},{3,2},{4,5},{5,4},{6,7},{7,6},{8,9},{9,8},{10,11... | collective-permute-start | bytes 393224 | tf_op jit(solution)/shard_map/ppermute | solution.py:32
  51.3 4.7 %collective-permute-start.17 = (f32[32,512]{1,0:T(8,128)S(1)}, f32[32,512]{1,0:T(8,128)S(1)}, u32[]{:S(2)}, u32[]{:S(2)}) collective-permute-start(f32[32,512]{1,0:T(8,128)S(1)} %add.48), channel_id=1, source_target_pairs={{0,16},{8,24},{16,0},{24,8},{1,17},{9,25},{17,1},{25,9},{2,18},{10... | collective-permute-start | bytes 196616 | tf_op jit(solution)/shard_map/ppermute | solution.py:32
  53.2 8.1 %collective-permute-start.13 = (f32[1,4,32,512]{3,2,1,0:T(8,128)S(1)}, f32[1,4,32,512]{3,2,1,0:T(8,128)S(1)}, u32[]{:S(2)}, u32[]{:S(2)}) collective-permute-start(f32[1,4,32,512]{3,2,1,0:T(8,128)S(1)} %bitcast.158), channel_id=1, source_target_pairs={{0,16},{8,24},{16,0},{24,8},{1,17},{9,25},{17,1},{25,9},{2,18},{10... | collective-permute-start | bytes 786440 | tf_op jit(solution)/shard_map/ppermute | solution.py:32
  56.0 12.9 %collective-permute-start.21 = (f32[1,32,512]{2,1,0:T(8,128)S(1)}, f32[1,32,512]{2,1,0:T(8,128)S(1)}, u32[]{:S(2)}, u32[]{:S(2)}) collective-permute-start(f32[1,32,512]{2,1,0:T(8,128)S(1)} %add_bitcast_fusion.refs_0_), channel_id=1, source_target_pairs={{0,3},{1,2},{2,1},{3,0},{4,7},{5,6},{6,5},{7,4},{8,11},{9,10},{10,... | collective-permute-start | bytes 196616 | tf_op jit(solution)/shard_map/ppermute | solution.py:32
  57.0 10.0 %collective-permute-start.20 = (f32[5,32,512]{2,1,0:T(8,128)S(1)}, f32[5,32,512]{2,1,0:T(8,128)S(1)}, u32[]{:S(2)}, u32[]{:S(2)}) collective-permute-start(f32[5,32,512]{2,1,0:T(8,128)S(1)} %get-tuple-element.91), channel_id=1, source_target_pairs={{0,2},{1,3},{2,0},{3,1},{4,6},{5,7},{6,4},{7,5},{8,10},{9,11},{10,... | collective-permute-start | bytes 983048 | tf_op jit(solution)/shard_map/ppermute | solution.py:32
  58.8 9.1 %collective-permute-start.18 = (f32[5,32,512]{2,1,0:T(8,128)S(1)}, f32[5,32,512]{2,1,0:T(8,128)S(1)}, u32[]{:S(2)}, u32[]{:S(2)}) collective-permute-start(f32[5,32,512]{2,1,0:T(8,128)S(1)} %get-tuple-element.92), channel_id=1, source_target_pairs={{0,1},{1,0},{2,3},{3,2},{4,5},{5,4},{6,7},{7,6},{8,9},{9,8},{10,11... | collective-permute-start | bytes 983048 | tf_op jit(solution)/shard_map/ppermute | solution.py:32
  61.4 6.8 %collective-permute-start.14 = (f32[2,4,32,512]{3,2,1,0:T(8,128)S(1)}, f32[2,4,32,512]{3,2,1,0:T(8,128)S(1)}, u32[]{:S(2)}, u32[]{:S(2)}) collective-permute-start(f32[2,4,32,512]{3,2,1,0:T(8,128)S(1)} %maximum_bitcast_fusion), channel_id=1, source_target_pairs={{0,8},{8,0},{16,24},{24,16},{1,9},{9,1},{17,25},{25,17},{2,10},{10... | collective-permute-start | bytes 1572872 | tf_op jit(solution)/shard_map/ppermute | solution.py:32
  68.3 1.6 %copy-start.1 = (f32[8,1,128,4,1,128]{5,4,3,2,1,0:T(1,128)S(1)}, f32[8,1,128,4,1,128]{5,4,3,2,1,0:T(1,128)}, u32[]{:S(2)}) copy-start(f32[8,1,128,4,1,128]{5,4,3,2,1,0:T(1,128)} %param.3) | copy-start | bytes 6291460

commit v2 on v1

--- a/solution.py
+++ b/solution.py
@@ -133,17 +133,14 @@
 def update_kernel(
     orders, inner_upper, a_ref, ur_ref, uc_ref, zc_ref, first_ref, second_ref, *refs
 ):
-    inners, (out_ref, inner, w, zt, block, result, read, write) = refs[:4], refs[4:]
+    inners, (out_ref, inner, w, zt, result, write) = refs[:4], refs[4:]
     near = lax.axis_index("pcol") & 3
     ratio, nb, cols = zt.shape
     nc, half = first_ref.shape[:2]
     slots = nc // ratio
-    chunks, lines, tile = block.shape
+    chunks, lines, tile = result.shape
     col_tiles = cols // tile
-    reads = [pltpu.make_async_copy(a_ref.at[pl.ds(i * lines, lines)], block.at[i], read.at[i]) for i in range(chunks)]
     writes = [pltpu.make_async_copy(result.at[i], out_ref.at[pl.ds(i * lines, lines)], write.at[i]) for i in range(chunks)]
-    for copy in reads:
-        copy.start()
     for g in range(ratio):
         for s in range(slots):
             for side, (ref, masks) in enumerate(zip((first_ref, second_ref), orders)):
@@ -161,11 +158,11 @@
         at = slice(i * rows, (i + 1) * rows)
         turned = [zt[g, :, b * tile : (b + 1) * tile].T for b in range(i * count, (i + 1) * count) for g in range(ratio)]
         total = dot(stack_left(jnp.concatenate(turned, axis=0)), uc_ref[...]) + dot(ur_ref[at, :], w[...])
-        reads[i].wait()
         for g in range(ratio * count):
             for b in range(col_tiles):
-                line = pl.ds(g * tile * col_tiles + b, tile, stride=col_tiles)
-                result[i, line, :] = block[i, line, :] - total[g * tile : (g + 1) * tile, b * tile : (b + 1) * tile]
+                at = g * tile * col_tiles + b
+                values = a_ref[pl.ds(i * lines + at, tile, stride=col_tiles), :]
+                result[i, pl.ds(at, tile, stride=col_tiles), :] = values - total[g * tile : (g + 1) * tile, b * tile : (b + 1) * tile]
         writes[i].start()
     for copy in writes:
         copy.wait()
@@ -279,8 +276,10 @@
     )(turned, y_rows)
     first, second = turned[None, : part // 2], turned[None, part // 2 :]
     first, second = lax.optimization_barrier(first), lax.optimization_barrier(second)
+    columns = jnp.concatenate([piece.reshape(2, part // 2, cols), y_cols])
     for mask in lead:
         first = join(first, swap(first, "pcol", mask), col[mask])
+        first, columns = lax.optimization_barrier((first, columns))
         came = swap(jnp.concatenate([second, inner[None]]), "pcol", mask)
         second, inner = join(second, came[:-1], col[mask]), inner + came[-1]
     for mask in rest[:-2]:
@@ -288,21 +287,16 @@
         second = join(second, swap(second, "pcol", mask), col[mask])
     first = join(first, swap(first, "pcol", far), col[far])
     second = join(second, swap(second, "pcol", close), col[close])
-
-    columns = jnp.concatenate([piece.reshape(2, part // 2, cols), y_cols])
+    first, inner = lax.optimization_barrier((first, inner))
+
     for mask in cols_order[::-1]:
         inner = inner + swap(inner, "prow", mask)
-        if mask == 1:
-            columns, inner = lax.optimization_barrier((columns, inner))
     inner = inner[None]
     for mask in rest[:-2]:
         inner = join(inner, swap(inner, "pcol", mask), col[mask])
-    first_came = swap(jnp.concatenate([first, inner]), "pcol", close)
-    second_came = swap(jnp.concatenate([second, inner]), "pcol", far)
-    blocks = first.shape[0]
-    near_inner = [inner, first_came[blocks:], second_came[blocks:], swap(inner, "pcol", close + far)]
-    first = join(first, first_came[:blocks], col[close])
-    second = join(second, second_came[:blocks], col[far])
+    near_inner = [inner] + [swap(inner, "pcol", mask) for mask in (close, far, close + far)]
+    first = join(first, swap(first, "pcol", close), col[close])
+    second = join(second, swap(second, "pcol", far), col[far])
 
     columns = gather(columns, "prow", cols_order, row)
     u_cols, zc = pl.pallas_call(
@@ -321,15 +315,13 @@
     result = pl.pallas_call(
         functools.partial(update_kernel, orders, inner_upper),
         out_shape=shape(rows * col_tiles, tile),
-        in_specs=[outside] + [whole] * 9,
+        in_specs=[whole] * 10,
         out_specs=outside,
         scratch_shapes=[
             pltpu.VMEM((nb, nb), F32),
             pltpu.VMEM((3 * nb, cols), BF16),
             pltpu.VMEM((ratio, nb, cols), F32),
             pltpu.VMEM((chunks, lines, tile), F32),
-            pltpu.VMEM((chunks, lines, tile), F32),
-            pltpu.SemaphoreType.DMA((chunks,)),
             pltpu.SemaphoreType.DMA((chunks,)),
         ],
         compiler_params=VMEM,

time: 74 us -> 71.2 us (0.962)
  waiting for transfers between devices: 28 us -> 20.9 us
  starting transfers between devices: 33.3 us -> 38.9 us
  Pallas kernels: 7.26 us -> 6.42 us
    ppermute x19 -> x21, waiting for transfers between devices: 28 us -> 20.9 us  [swap(): return lax.ppermute(values, axis, [(i, i ^ mask) for i in range(n)])]
    ppermute x19 -> x21, starting transfers between devices: 28.2 us -> 33.7 us  [swap(): return lax.ppermute(values, axis, [(i, i ^ mask) for i in range(n)])]
    pallas_call x1, Pallas kernels: 3.83 us -> 2.98 us  [per_device(): pl.pallas_call(functools.partial(update_kernel, orders, inner_upper), out...]
  transfers between devices with their start and end apart: 22 -> 24, of which waited for: 15 -> 16; matrix products, arithmetic and copies ran while one was open for 2% -> 1% of each run, Pallas kernels for 3% -> 3%
where the time goes in v2:
time: 71.2 us; the launch traced here: 71 us
  starting transfers between devices  38.9 us (55%)
  waiting for transfers between devices  20.9 us (29%)
  Pallas kernels  6.42 us (9%)
  local copies, waits for them, and re-layouts  3.34 us (5%)
  other arithmetic  1.04 us (1%)
    ppermute x21, starting transfers between devices, swap(): return lax.ppermute(values, axis, [(i, i ^ mask) for i in range(n)])  33.7 us
    ppermute x21, waiting for transfers between devices, swap(): return lax.ppermute(values, axis, [(i, i ^ mask) for i in range(n)])  20.9 us
    ppermute x3, starting transfers between devices, turn(): return lax.ppermute(values, BOTH, perm)  5.16 us
    pallas_call x1, Pallas kernels, per_device(): pl.pallas_call(functools.partial(update_kernel, orders, inner_upper), out...  2.98 us
    unnamed x6, local copies, waits for them, and re-layouts  2.38 us
  transfers between devices with their start and end apart: 24, of which 16 were waited for; matrix products, arithmetic and copies ran while one was open for 1% of the time, Pallas kernels for 3%

profile of v2, /device:TPU:0, one launch (start us, length us, event | category | flops | bytes accessed | tf_op | source)
XLA Modules:
  0.0 71.0 jit_solution(547705816943754516)
XLA Ops:
  0.0 0.9 %slice_bitcast_fusion.3 = (f32[1,4,32,128]{3,2,1,0:T(8,128)S(1)}, f32[1,4,32,128]{3,2,1,0:T(8,128)S(1)}) fusion(f32[8,32,128]{2,1,0:T(8,128)} %bitcast.157), kind=kLoop, calls=%fused_computation.54 | loop fusion | bytes 262144 | tf_op jit(solution)/shard_map/broadcast_in_dim | solution.py:224
  0.9 4.1 %collective-permute-start.1 = (f32[1,4,32,128]{3,2,1,0:T(8,128)S(1)}, f32[1,4,32,128]{3,2,1,0:T(8,128)S(1)}, u32[]{:S(2)}, u32[]{:S(2)}) collective-permute-start(f32[1,4,32,128]{3,2,1,0:T(8,128)S(1)} %get-tuple-element.93), channel_id=1, source_target_pairs={{0,4},{1,5},{2,6},{3,7},{4,0},{5,1},{6,2},{7,3},{8,12},{9,13},{10,... | collective-permute-start | bytes 196616 | tf_op jit(solution)/shard_map/ppermute | solution.py:32
  5.0 0.1 collective-permute-start
  5.1 1.6 %copy-done = f32[8,1,128,4,1,128]{5,4,3,2,1,0:T(1,128)S(1)} copy-done((f32[8,1,128,4,1,128]{5,4,3,2,1,0:T(1,128)S(1)}, f32[8,1,128,4,1,128]{5,4,3,2,1,0:T(1,128)}, u32[]{:S(2)}) %copy-start) | copy-done | bytes 2097176
  6.7 0.5 shard_map.37
  7.2 1.5 %collective-permute-done.1 = f32[1,4,32,128]{3,2,1,0:T(8,128)S(1)} collective-permute-done((f32[1,4,32,128]{3,2,1,0:T(8,128)S(1)}, f32[1,4,32,128]{3,2,1,0:T(8,128)S(1)}, u32[]{:S(2)}, u32[]{:S(2)}) %collective-permute-start.1) | collective-permute-done | bytes 65568 | tf_op jit(solution)/shard_map/ppermute | solution.py:32
  8.7 2.1 %collective-permute-start.2 = (f32[2,4,32,128]{3,2,1,0:T(8,128)S(1)}, f32[2,4,32,128]{3,2,1,0:T(8,128)S(1)}, u32[]{:S(2)}, u32[]{:S(2)}) collective-permute-start(f32[2,4,32,128]{3,2,1,0:T(8,128)S(1)} %maximum_bitcast_fusion.1), channel_id=1, source_target_pairs={{0,2},{1,3},{2,0},{3,1},{4,6},{5,7},{6,4},{7,5},{8,10},{9,11},{10,... | collective-permute-start | bytes 393224 | tf_op jit(solution)/shard_map/ppermute | solution.py:32
  10.8 0.6 collective-permute-done
  11.5 1.8 %collective-permute-start.4 = (f32[2,4,32,128]{3,2,1,0:T(8,128)S(1)}, f32[2,4,32,128]{3,2,1,0:T(8,128)S(1)}, u32[]{:S(2)}, u32[]{:S(2)}) collective-permute-start(f32[2,4,32,128]{3,2,1,0:T(8,128)S(1)} %maximum_bitcast_fusion.2), channel_id=1, source_target_pairs={{0,1},{1,0},{2,3},{3,2},{4,5},{5,4},{6,7},{7,6},{8,9},{9,8},{10,11... | collective-permute-start | bytes 393224 | tf_op jit(solution)/shard_map/ppermute | solution.py:32
  13.2 1.1 %collective-permute-done.2 = f32[2,4,32,128]{3,2,1,0:T(8,128)S(1)} collective-permute-done((f32[2,4,32,128]{3,2,1,0:T(8,128)S(1)}, f32[2,4,32,128]{3,2,1,0:T(8,128)S(1)}, u32[]{:S(2)}, u32[]{:S(2)}) %collective-permute-start.2) | collective-permute-done | bytes 131104 | tf_op jit(solution)/shard_map/ppermute | solution.py:32
  14.4 1.6 %collective-permute-start.3 = (f32[4,4,32,128]{3,2,1,0:T(8,128)S(1)}, f32[4,4,32,128]{3,2,1,0:T(8,128)S(1)}, u32[]{:S(2)}, u32[]{:S(2)}) collective-permute-start(f32[4,4,32,128]{3,2,1,0:T(8,128)S(1)} %bitcast.154), channel_id=1, source_target_pairs={{0,1},{1,0},{2,3},{3,2},{4,5},{5,4},{6,7},{7,6},{8,9},{9,8},{10,11... | collective-permute-start | bytes 786440 | tf_op jit(solution)/shard_map/ppermute | solution.py:32
  16.1 0.8 %collective-permute-done.4 = f32[2,4,32,128]{3,2,1,0:T(8,128)S(1)} collective-permute-done((f32[2,4,32,128]{3,2,1,0:T(8,128)S(1)}, f32[2,4,32,128]{3,2,1,0:T(8,128)S(1)}, u32[]{:S(2)}, u32[]{:S(2)}) %collective-permute-start.4) | collective-permute-done | bytes 131104 | tf_op jit(solution)/shard_map/ppermute | solution.py:32
  17.0 0.9 %collective-permute-start.5 = (f32[4,4,32,128]{3,2,1,0:T(8,128)S(1)}, f32[4,4,32,128]{3,2,1,0:T(8,128)S(1)}, u32[]{:S(2)}, u32[]{:S(2)}) collective-permute-start(f32[4,4,32,128]{3,2,1,0:T(8,128)S(1)} %bitcast.155), channel_id=1, source_target_pairs={{0,2},{1,3},{2,0},{3,1},{4,6},{5,7},{6,4},{7,5},{8,10},{9,11},{10,... | collective-permute-start | bytes 786440 | tf_op jit(solution)/shard_map/ppermute | solution.py:32
  17.9 4.5 %collective-permute-done.3 = f32[4,4,32,128]{3,2,1,0:T(8,128)S(1)} collective-permute-done((f32[4,4,32,128]{3,2,1,0:T(8,128)S(1)}, f32[4,4,32,128]{3,2,1,0:T(8,128)S(1)}, u32[]{:S(2)}, u32[]{:S(2)}) %collective-permute-start.3) | collective-permute-done | bytes 262176 | tf_op jit(solution)/shard_map/ppermute | solution.py:32
  22.3 1.6 %collective-permute-done.5 = f32[4,4,32,128]{3,2,1,0:T(8,128)S(1)} collective-permute-done((f32[4,4,32,128]{3,2,1,0:T(8,128)S(1)}, f32[4,4,32,128]{3,2,1,0:T(8,128)S(1)}, u32[]{:S(2)}, u32[]{:S(2)}) %collective-permute-start.5) | collective-permute-done | bytes 262176 | tf_op jit(solution)/shard_map/ppermute | solution.py:32
  23.9 0.1 select_bitcast_fusion.9
  24.2 0.0 copy-start.2
  24.2 1.1 %shard_map.38 = (f32[8,256,128]{2,1,0:T(8,128)S(1)}, f32[2,64,512]{2,1,0:T(8,128)S(1)}, f32[2,64,512]{2,1,0:T(8,128)S(1)}) custom-call(bf16[1024,512]{1,0:T(8,128)(2,1)S(1)} %get-tuple-element.36.ah_ref, bf16[1024,512]{1,0:T(8,128)(2,1)S(1)} %get-tuple-element.37.al_ref, f32[8,4,32,128]{3,2,1,0:T(8,128)S(1)} %bitcast.148, f32[8,4,32,128]{3,2,1,0:T(8,128)S(1)} %bitcast.147), custom_call_target="tpu_custom_call" | custom-call | flops 805306368 | bytes 4194304 | tf_op jit(solution)/shard_map/pallas_call | solution.py:231
  25.2 0.1 collective-permute-start.6
  25.4 0.7 collective-permute-start.11
  26.0 0.8 %collective-permute-done.6 = f32[2,64,512]{2,1,0:T(8,128)S(1)} collective-permute-done((f32[2,64,512]{2,1,0:T(8,128)S(1)}, f32[2,64,512]{2,1,0:T(8,128)S(1)}, u32[]{:S(2)}, u32[]{:S(2)}) %collective-permute-start.6) | collective-permute-done | bytes 262176 | tf_op jit(solution)/shard_map/ppermute | solution.py:32
  26.9 3.8 %collective-permute-start.8 = (f32[64,512]{1,0:T(8,128)S(1)}, f32[64,512]{1,0:T(8,128)S(1)}, u32[]{:S(2)}, u32[]{:S(2)}) collective-permute-start(f32[64,512]{1,0:T(8,128)S(1)} %get-tuple-element.77), channel_id=1, source_target_pairs={{0,2},{1,10},{2,18},{3,26},{4,6},{5,14},{6,22},{7,30},{8,3},{9,11}... | collective-permute-start | bytes 393224 | tf_op jit(solution)/shard_map/ppermute | solution.py:211
  30.8 0.7 collective-permute-start.7
  31.4 0.0 copy-done.2
  31.4 1.0 %shard_map.39.ur_ref = bf16[1024,768]{1,0:T(8,128)(2,1)S(1)} custom-call(f32[256,256]{1,0:T(8,128)S(1)} %copy-done.2, f32[8,256,128]{2,1,0:T(8,128)S(1)} %get-tuple-element.46.y_ref), custom_call_target="tpu_custom_call" | custom-call | flops 402653184 | bytes 2097152 | tf_op jit(solution)/shard_map/pallas_call | solution.py:260
  32.5 2.8 %collective-permute-start.10 = (f32[1,64,512]{2,1,0:T(8,128)S(1)}, f32[1,64,512]{2,1,0:T(8,128)S(1)}, u32[]{:S(2)}, u32[]{:S(2)}) collective-permute-start(f32[1,64,512]{2,1,0:T(8,128)S(1)} %constant_dynamic-slice_fusion), channel_id=1, source_target_pairs={{0,16},{8,24},{16,0},{24,8},{1,17},{9,25},{17,1},{25,9},{2,18},{10... | collective-permute-start | bytes 393224 | tf_op jit(solution)/shard_map/ppermute | solution.py:32
  35.3 0.0 collective-permute-done.8
  35.3 0.0 collective-permute-done.7
  35.4 2.6 %collective-permute-start.9 = (f32[1,32,512]{2,1,0:T(8,128)S(1)}, f32[1,32,512]{2,1,0:T(8,128)S(1)}, u32[]{:S(2)}, u32[]{:S(2)}) collective-permute-start(f32[1,32,512]{2,1,0:T(8,128)S(1)} %get-tuple-element.86), channel_id=1, source_target_pairs={{0,4},{1,5},{2,6},{3,7},{4,0},{5,1},{6,2},{7,3},{8,12},{9,13},{10,... | collective-permute-start | bytes 196616 | tf_op jit(solution)/shard_map/ppermute | solution.py:32
  37.9 0.4 shard_map.41
  38.3 0.5 collective-permute-start.15
  38.8 1.2 %collective-permute-done.10 = f32[1,64,512]{2,1,0:T(8,128)S(1)} collective-permute-done((f32[1,64,512]{2,1,0:T(8,128)S(1)}, f32[1,64,512]{2,1,0:T(8,128)S(1)}, u32[]{:S(2)}, u32[]{:S(2)}) %collective-permute-start.10) | collective-permute-done | bytes 131104 | tf_op jit(solution)/shard_map/ppermute | solution.py:32
  40.0 0.0 collective-permute-done.11
  40.1 0.5 collective-permute-done.9
  40.6 4.9 %collective-permute-start.14 = (f32[2,32,512]{2,1,0:T(8,128)S(1)}, f32[2,32,512]{2,1,0:T(8,128)S(1)}, u32[]{:S(2)}, u32[]{:S(2)}) collective-permute-start(f32[2,32,512]{2,1,0:T(8,128)S(1)} %maximum_bitcast_fusion.3), channel_id=1, source_target_pairs={{0,2},{1,3},{2,0},{3,1},{4,6},{5,7},{6,4},{7,5},{8,10},{9,11},{10,... | collective-permute-start | bytes 393224 | tf_op jit(solution)/shard_map/ppermute | solution.py:32
  45.5 4.0 %collective-permute-start.12 = (f32[1,4,32,512]{3,2,1,0:T(8,128)S(1)}, f32[1,4,32,512]{3,2,1,0:T(8,128)S(1)}, u32[]{:S(2)}, u32[]{:S(2)}) collective-permute-start(f32[1,4,32,512]{3,2,1,0:T(8,128)S(1)} %bitcast.150), channel_id=1, source_target_pairs={{0,16},{8,24},{16,0},{24,8},{1,17},{9,25},{17,1},{25,9},{2,18},{10... | collective-permute-start | bytes 786440 | tf_op jit(solution)/shard_map/ppermute | solution.py:32
  49.5 0.3 collective-permute-done.15
  49.8 1.1 %collective-permute-start.17 = (f32[2,32,512]{2,1,0:T(8,128)S(1)}, f32[2,32,512]{2,1,0:T(8,128)S(1)}, u32[]{:S(2)}, u32[]{:S(2)}) collective-permute-start(f32[2,32,512]{2,1,0:T(8,128)S(1)} %maximum_bitcast_fusion.4), channel_id=1, source_target_pairs={{0,1},{1,0},{2,3},{3,2},{4,5},{5,4},{6,7},{7,6},{8,9},{9,8},{10,11... | collective-permute-start | bytes 393224 | tf_op jit(solution)/shard_map/ppermute | solution.py:32
  50.9 0.0 collective-permute-done.14
  51.0 1.9 %collective-permute-start.19 = (f32[32,512]{1,0:T(8,128)S(1)}, f32[32,512]{1,0:T(8,128)S(1)}, u32[]{:S(2)}, u32[]{:S(2)}) collective-permute-start(f32[32,512]{1,0:T(8,128)S(1)} %fusion), channel_id=1, source_target_pairs={{0,8},{8,0},{16,24},{24,16},{1,9},{9,1},{17,25},{25,17},{2,10},{10... | collective-permute-start | bytes 196616 | tf_op jit(solution)/shard_map/ppermute | solution.py:32
  52.9 0.1 collective-permute-start.16
  53.0 3.2 %collective-permute-done.17 = f32[2,32,512]{2,1,0:T(8,128)S(1)} collective-permute-done((f32[2,32,512]{2,1,0:T(8,128)S(1)}, f32[2,32,512]{2,1,0:T(8,128)S(1)}, u32[]{:S(2)}, u32[]{:S(2)}) %collective-permute-start.17) | collective-permute-done | bytes 131104 | tf_op jit(solution)/shard_map/ppermute | solution.py:32
  56.3 0.0 collective-permute-done.19
  56.3 0.9 %collective-permute-start.20 = (f32[32,512]{1,0:T(8,128)S(1)}, f32[32,512]{1,0:T(8,128)S(1)}, u32[]{:S(2)}, u32[]{:S(2)}) collective-permute-start(f32[32,512]{1,0:T(8,128)S(1)} %add.48), channel_id=1, source_target_pairs={{0,16},{8,24},{16,0},{24,8},{1,17},{9,25},{17,1},{25,9},{2,18},{10... | collective-permute-start | bytes 196616 | tf_op jit(solution)/shard_map/ppermute | solution.py:32
  57.2 0.6 collective-permute-start.18
  57.9 2.8 %collective-permute-done.20 = f32[32,512]{1,0:T(8,128)S(1)} collective-permute-done((f32[32,512]{1,0:T(8,128)S(1)}, f32[32,512]{1,0:T(8,128)S(1)}, u32[]{:S(2)}, u32[]{:S(2)}) %collective-permute-start.20) | collective-permute-done | bytes 65568 | tf_op jit(solution)/shard_map/ppermute | solution.py:32
  60.7 0.4 collective-permute-start.23
  61.0 1.2 %collective-permute-start.22 = (f32[1,32,512]{2,1,0:T(8,128)S(1)}, f32[1,32,512]{2,1,0:T(8,128)S(1)}, u32[]{:S(2)}, u32[]{:S(2)}) collective-permute-start(f32[1,32,512]{2,1,0:T(8,128)S(1)} %add_bitcast_fusion.refs_0_), channel_id=1, source_target_pairs={{0,2},{1,3},{2,0},{3,1},{4,6},{5,7},{6,4},{7,5},{8,10},{9,11},{10,... | collective-permute-start | bytes 196616 | tf_op jit(solution)/shard_map/ppermute | solution.py:32
  62.3 0.0 collective-permute-done.12
  62.3 1.9 %collective-permute-start.21 = (f32[1,32,512]{2,1,0:T(8,128)S(1)}, f32[1,32,512]{2,1,0:T(8,128)S(1)}, u32[]{:S(2)}, u32[]{:S(2)}) collective-permute-start(f32[1,32,512]{2,1,0:T(8,128)S(1)} %add_bitcast_fusion.refs_0_), channel_id=1, source_target_pairs={{0,1},{1,0},{2,3},{3,2},{4,5},{5,4},{6,7},{7,6},{8,9},{9,8},{10,11... | collective-permute-start | bytes 196616 | tf_op jit(solution)/shard_map/ppermute | solution.py:32
  64.3 0.0 collective-permute-done.16
  64.3 0.1 collective-permute-start.13
  64.5 1.2 %collective-permute-done.18 = f32[4,32,512]{2,1,0:T(8,128)S(1)} collective-permute-done((f32[4,32,512]{2,1,0:T(8,128)S(1)}, f32[4,32,512]{2,1,0:T(8,128)S(1)}, u32[]{:S(2)}, u32[]{:S(2)}) %collective-permute-start.18) | collective-permute-done | bytes 262176 | tf_op jit(solution)/shard_map/ppermute | solution.py:32
  65.7 0.1 select_bitcast_fusion.3
  65.8 0.5 collective-permute-done.13
  66.3 0.1 select_bitcast_fusion.1
  66.4 0.0 copy-start.1
  66.4 0.1 pad_maximum_fusion
  66.5 0.4 shard_map.40
  67.0 0.0 collective-permute-done.23.refs_3_
  67.0 0.1 collective-permute-done.22.refs_2_
  67.1 0.2 collective-permute-done.21.refs_1_
  67.2 0.8 %copy-done.1 = f32[8,1,128,4,1,128]{5,4,3,2,1,0:T(1,128)S(1)} copy-done((f32[8,1,128,4,1,128]{5,4,3,2,1,0:T(1,128)S(1)}, f32[8,1,128,4,1,128]{5,4,3,2,1,0:T(1,128)}, u32[]{:S(2)}) %copy-start.1) | copy-done | bytes 2097176
  68.0 3.0 %shard_map.42 = f32[4096,128]{1,0:T(8,128)} custom-call(f32[4096,128]{1,0:T(8,128)S(1)} %bitcast.142, bf16[1024,768]{1,0:T(8,128)(2,1)S(1)} %shard_map.39.ur_ref, bf16[768,512]{1,0:T(8,128)(2,1)S(1)} %get-tuple-element.56.uc_ref, f32[256,512]{1,0:T(8,128)S(1)} %get-tuple-element.57.zc_ref, f32[8,32,512]{2,1,0:T(8,128)S(1)} %bitcast.145, ...), custom_call_target="tpu_custom_call" | custom-call | flops 1610612736 | bytes 4194304 | tf_op jit(solution)/shard_map/pallas_call | solution.py:315
  (36 shorter events, 0.7 us)
Async XLA Ops:
  0.9 7.8 %collective-permute-start.1 = (f32[1,4,32,128]{3,2,1,0:T(8,128)S(1)}, f32[1,4,32,128]{3,2,1,0:T(8,128)S(1)}, u32[]{:S(2)}, u32[]{:S(2)}) collective-permute-start(f32[1,4,32,128]{3,2,1,0:T(8,128)S(1)} %get-tuple-element.93), channel_id=1, source_target_pairs={{0,4},{1,5},{2,6},{3,7},{4,0},{5,1},{6,2},{7,3},{8,12},{9,13},{10,... | collective-permute-start | bytes 196616 | tf_op jit(solution)/shard_map/ppermute | solution.py:32
  5.0 6.5 %collective-permute-start = (f32[1,4,32,128]{3,2,1,0:T(8,128)S(1)}, f32[1,4,32,128]{3,2,1,0:T(8,128)S(1)}, u32[]{:S(2)}, u32[]{:S(2)}) collective-permute-start(f32[1,4,32,128]{3,2,1,0:T(8,128)S(1)} %get-tuple-element.94), channel_id=1, source_target_pairs={{0,4},{1,5},{2,6},{3,7},{4,0},{5,1},{6,2},{7,3},{8,12},{9,13},{10,... | collective-permute-start | bytes 196616 | tf_op jit(solution)/shard_map/ppermute | solution.py:32
  5.1 1.6 %copy-start = (f32[8,1,128,4,1,128]{5,4,3,2,1,0:T(1,128)S(1)}, f32[8,1,128,4,1,128]{5,4,3,2,1,0:T(1,128)}, u32[]{:S(2)}) copy-start(f32[8,1,128,4,1,128]{5,4,3,2,1,0:T(1,128)} %param.3) | copy-start | bytes 6291460
  8.7 5.7 %collective-permute-start.2 = (f32[2,4,32,128]{3,2,1,0:T(8,128)S(1)}, f32[2,4,32,128]{3,2,1,0:T(8,128)S(1)}, u32[]{:S(2)}, u32[]{:S(2)}) collective-permute-start(f32[2,4,32,128]{3,2,1,0:T(8,128)S(1)} %maximum_bitcast_fusion.1), channel_id=1, source_target_pairs={{0,2},{1,3},{2,0},{3,1},{4,6},{5,7},{6,4},{7,5},{8,10},{9,11},{10,... | collective-permute-start | bytes 393224 | tf_op jit(solution)/shard_map/ppermute | solution.py:32
  11.5 5.4 %collective-permute-start.4 = (f32[2,4,32,128]{3,2,1,0:T(8,128)S(1)}, f32[2,4,32,128]{3,2,1,0:T(8,128)S(1)}, u32[]{:S(2)}, u32[]{:S(2)}) collective-permute-start(f32[2,4,32,128]{3,2,1,0:T(8,128)S(1)} %maximum_bitcast_fusion.2), channel_id=1, source_target_pairs={{0,1},{1,0},{2,3},{3,2},{4,5},{5,4},{6,7},{7,6},{8,9},{9,8},{10,11... | collective-permute-start | bytes 393224 | tf_op jit(solution)/shard_map/ppermute | solution.py:32
  14.4 7.9 %collective-permute-start.3 = (f32[4,4,32,128]{3,2,1,0:T(8,128)S(1)}, f32[4,4,32,128]{3,2,1,0:T(8,128)S(1)}, u32[]{:S(2)}, u32[]{:S(2)}) collective-permute-start(f32[4,4,32,128]{3,2,1,0:T(8,128)S(1)} %bitcast.154), channel_id=1, source_target_pairs={{0,1},{1,0},{2,3},{3,2},{4,5},{5,4},{6,7},{7,6},{8,9},{9,8},{10,11... | collective-permute-start | bytes 786440 | tf_op jit(solution)/shard_map/ppermute | solution.py:32
  17.0 7.0 %collective-permute-start.5 = (f32[4,4,32,128]{3,2,1,0:T(8,128)S(1)}, f32[4,4,32,128]{3,2,1,0:T(8,128)S(1)}, u32[]{:S(2)}, u32[]{:S(2)}) collective-permute-start(f32[4,4,32,128]{3,2,1,0:T(8,128)S(1)} %bitcast.155), channel_id=1, source_target_pairs={{0,2},{1,3},{2,0},{3,1},{4,6},{5,7},{6,4},{7,5},{8,10},{9,11},{10,... | collective-permute-start | bytes 786440 | tf_op jit(solution)/shard_map/ppermute | solution.py:32
  24.2 7.3 %copy-start.2 = (f32[256,256]{1,0:T(8,128)S(1)}, f32[256,256]{1,0:T(8,128)}, u32[]{:S(2)}) copy-start(f32[256,256]{1,0:T(8,128)} %t_ref.3) | copy-start | bytes 786436
  25.2 1.6 %collective-permute-start.6 = (f32[2,64,512]{2,1,0:T(8,128)S(1)}, f32[2,64,512]{2,1,0:T(8,128)S(1)}, u32[]{:S(2)}, u32[]{:S(2)}) collective-permute-start(f32[2,64,512]{2,1,0:T(8,128)S(1)} %get-tuple-element.43), channel_id=1, source_target_pairs={{0,8},{8,0},{16,24},{24,16},{1,9},{9,1},{17,25},{25,17},{2,10},{10... | collective-permute-start | bytes 786440 | tf_op jit(solution)/shard_map/ppermute | solution.py:32
  25.4 14.7 %collective-permute-start.11 = (f32[64,512]{1,0:T(8,128)S(1)}, f32[64,512]{1,0:T(8,128)S(1)}, u32[]{:S(2)}, u32[]{:S(2)}) collective-permute-start(f32[64,512]{1,0:T(8,128)S(1)} %copy_bitcast_fusion), channel_id=1, source_target_pairs={{0,0},{1,8},{2,16},{3,24},{4,4},{5,12},{6,20},{7,28},{8,1},{9,9},{... | collective-permute-start | bytes 393224 | tf_op jit(solution)/shard_map/ppermute | solution.py:211
  26.9 8.4 %collective-permute-start.8 = (f32[64,512]{1,0:T(8,128)S(1)}, f32[64,512]{1,0:T(8,128)S(1)}, u32[]{:S(2)}, u32[]{:S(2)}) collective-permute-start(f32[64,512]{1,0:T(8,128)S(1)} %get-tuple-element.77), channel_id=1, source_target_pairs={{0,2},{1,10},{2,18},{3,26},{4,6},{5,14},{6,22},{7,30},{8,3},{9,11}... | collective-permute-start | bytes 393224 | tf_op jit(solution)/shard_map/ppermute | solution.py:211
  30.8 4.6 %collective-permute-start.7 = (f32[64,512]{1,0:T(8,128)S(1)}, f32[64,512]{1,0:T(8,128)S(1)}, u32[]{:S(2)}, u32[]{:S(2)}) collective-permute-start(f32[64,512]{1,0:T(8,128)S(1)} %get-tuple-element.78), channel_id=1, source_target_pairs={{0,0},{1,8},{2,16},{3,24},{4,4},{5,12},{6,20},{7,28},{8,1},{9,9},{... | collective-permute-start | bytes 393224 | tf_op jit(solution)/shard_map/ppermute | solution.py:211
  32.5 7.5 %collective-permute-start.10 = (f32[1,64,512]{2,1,0:T(8,128)S(1)}, f32[1,64,512]{2,1,0:T(8,128)S(1)}, u32[]{:S(2)}, u32[]{:S(2)}) collective-permute-start(f32[1,64,512]{2,1,0:T(8,128)S(1)} %constant_dynamic-slice_fusion), channel_id=1, source_target_pairs={{0,16},{8,24},{16,0},{24,8},{1,17},{9,25},{17,1},{25,9},{2,18},{10... | collective-permute-start | bytes 393224 | tf_op jit(solution)/shard_map/ppermute | solution.py:32
  35.4 5.2 %collective-permute-start.9 = (f32[1,32,512]{2,1,0:T(8,128)S(1)}, f32[1,32,512]{2,1,0:T(8,128)S(1)}, u32[]{:S(2)}, u32[]{:S(2)}) collective-permute-start(f32[1,32,512]{2,1,0:T(8,128)S(1)} %get-tuple-element.86), channel_id=1, source_target_pairs={{0,4},{1,5},{2,6},{3,7},{4,0},{5,1},{6,2},{7,3},{8,12},{9,13},{10,... | collective-permute-start | bytes 196616 | tf_op jit(solution)/shard_map/ppermute | solution.py:32
  38.3 11.4 %collective-permute-start.15 = (f32[2,32,512]{2,1,0:T(8,128)S(1)}, f32[2,32,512]{2,1,0:T(8,128)S(1)}, u32[]{:S(2)}, u32[]{:S(2)}) collective-permute-start(f32[2,32,512]{2,1,0:T(8,128)S(1)} %pad_maximum_fusion.10), channel_id=1, source_target_pairs={{0,4},{1,5},{2,6},{3,7},{4,0},{5,1},{6,2},{7,3},{8,12},{9,13},{10,... | collective-permute-start | bytes 393224 | tf_op jit(solution)/shard_map/ppermute | solution.py:32
  40.6 10.3 %collective-permute-start.14 = (f32[2,32,512]{2,1,0:T(8,128)S(1)}, f32[2,32,512]{2,1,0:T(8,128)S(1)}, u32[]{:S(2)}, u32[]{:S(2)}) collective-permute-start(f32[2,32,512]{2,1,0:T(8,128)S(1)} %maximum_bitcast_fusion.3), channel_id=1, source_target_pairs={{0,2},{1,3},{2,0},{3,1},{4,6},{5,7},{6,4},{7,5},{8,10},{9,11},{10,... | collective-permute-start | bytes 393224 | tf_op jit(solution)/shard_map/ppermute | solution.py:32
  45.5 16.8 %collective-permute-start.12 = (f32[1,4,32,512]{3,2,1,0:T(8,128)S(1)}, f32[1,4,32,512]{3,2,1,0:T(8,128)S(1)}, u32[]{:S(2)}, u32[]{:S(2)}) collective-permute-start(f32[1,4,32,512]{3,2,1,0:T(8,128)S(1)} %bitcast.150), channel_id=1, source_target_pairs={{0,16},{8,24},{16,0},{24,8},{1,17},{9,25},{17,1},{25,9},{2,18},{10... | collective-permute-start | bytes 786440 | tf_op jit(solution)/shard_map/ppermute | solution.py:32
  49.8 6.4 %collective-permute-start.17 = (f32[2,32,512]{2,1,0:T(8,128)S(1)}, f32[2,32,512]{2,1,0:T(8,128)S(1)}, u32[]{:S(2)}, u32[]{:S(2)}) collective-permute-start(f32[2,32,512]{2,1,0:T(8,128)S(1)} %maximum_bitcast_fusion.4), channel_id=1, source_target_pairs={{0,1},{1,0},{2,3},{3,2},{4,5},{5,4},{6,7},{7,6},{8,9},{9,8},{10,11... | collective-permute-start | bytes 393224 | tf_op jit(solution)/shard_map/ppermute | solution.py:32
  51.0 5.3 %collective-permute-start.19 = (f32[32,512]{1,0:T(8,128)S(1)}, f32[32,512]{1,0:T(8,128)S(1)}, u32[]{:S(2)}, u32[]{:S(2)}) collective-permute-start(f32[32,512]{1,0:T(8,128)S(1)} %fusion), channel_id=1, source_target_pairs={{0,8},{8,0},{16,24},{24,16},{1,9},{9,1},{17,25},{25,17},{2,10},{10... | collective-permute-start | bytes 196616 | tf_op jit(solution)/shard_map/ppermute | solution.py:32
  52.9 11.4 %collective-permute-start.16 = (f32[4,32,512]{2,1,0:T(8,128)S(1)}, f32[4,32,512]{2,1,0:T(8,128)S(1)}, u32[]{:S(2)}, u32[]{:S(2)}) collective-permute-start(f32[4,32,512]{2,1,0:T(8,128)S(1)} %bitcast.151), channel_id=1, source_target_pairs={{0,1},{1,0},{2,3},{3,2},{4,5},{5,4},{6,7},{7,6},{8,9},{9,8},{10,11... | collective-permute-start | bytes 786440 | tf_op jit(solution)/shard_map/ppermute | solution.py:32
  56.3 4.3 %collective-permute-start.20 = (f32[32,512]{1,0:T(8,128)S(1)}, f32[32,512]{1,0:T(8,128)S(1)}, u32[]{:S(2)}, u32[]{:S(2)}) collective-permute-start(f32[32,512]{1,0:T(8,128)S(1)} %add.48), channel_id=1, source_target_pairs={{0,16},{8,24},{16,0},{24,8},{1,17},{9,25},{17,1},{25,9},{2,18},{10... | collective-permute-start | bytes 196616 | tf_op jit(solution)/shard_map/ppermute | solution.py:32
  57.2 8.4 %collective-permute-start.18 = (f32[4,32,512]{2,1,0:T(8,128)S(1)}, f32[4,32,512]{2,1,0:T(8,128)S(1)}, u32[]{:S(2)}, u32[]{:S(2)}) collective-permute-start(f32[4,32,512]{2,1,0:T(8,128)S(1)} %bitcast.153), channel_id=1, source_target_pairs={{0,2},{1,3},{2,0},{3,1},{4,6},{5,7},{6,4},{7,5},{8,10},{9,11},{10,... | collective-permute-start | bytes 786440 | tf_op jit(solution)/shard_map/ppermute | solution.py:32
  60.7 6.3 %collective-permute-start.23 = (f32[1,32,512]{2,1,0:T(8,128)S(1)}, f32[1,32,512]{2,1,0:T(8,128)S(1)}, u32[]{:S(2)}, u32[]{:S(2)}) collective-permute-start(f32[1,32,512]{2,1,0:T(8,128)S(1)} %add_bitcast_fusion.refs_0_), channel_id=1, source_target_pairs={{0,3},{1,2},{2,1},{3,0},{4,7},{5,6},{6,5},{7,4},{8,11},{9,10},{10,... | collective-permute-start | bytes 196616 | tf_op jit(solution)/shard_map/ppermute | solution.py:32
  61.0 6.0 %collective-permute-start.22 = (f32[1,32,512]{2,1,0:T(8,128)S(1)}, f32[1,32,512]{2,1,0:T(8,128)S(1)}, u32[]{:S(2)}, u32[]{:S(2)}) collective-permute-start(f32[1,32,512]{2,1,0:T(8,128)S(1)} %add_bitcast_fusion.refs_0_), channel_id=1, source_target_pairs={{0,2},{1,3},{2,0},{3,1},{4,6},{5,7},{6,4},{7,5},{8,10},{9,11},{10,... | collective-permute-start | bytes 196616 | tf_op jit(solution)/shard_map/ppermute | solution.py:32
  62.3 5.0 %collective-permute-start.21 = (f32[1,32,512]{2,1,0:T(8,128)S(1)}, f32[1,32,512]{2,1,0:T(8,128)S(1)}, u32[]{:S(2)}, u32[]{:S(2)}) collective-permute-start(f32[1,32,512]{2,1,0:T(8,128)S(1)} %add_bitcast_fusion.refs_0_), channel_id=1, source_target_pairs={{0,1},{1,0},{2,3},{3,2},{4,5},{5,4},{6,7},{7,6},{8,9},{9,8},{10,11... | collective-permute-start | bytes 196616 | tf_op jit(solution)/shard_map/ppermute | solution.py:32
  64.3 2.0 %collective-permute-start.13 = (f32[2,4,32,512]{3,2,1,0:T(8,128)S(1)}, f32[2,4,32,512]{3,2,1,0:T(8,128)S(1)}, u32[]{:S(2)}, u32[]{:S(2)}) collective-permute-start(f32[2,4,32,512]{3,2,1,0:T(8,128)S(1)} %maximum_bitcast_fusion), channel_id=1, source_target_pairs={{0,8},{8,0},{16,24},{24,16},{1,9},{9,1},{17,25},{25,17},{2,10},{10... | collective-permute-start | bytes 1572872 | tf_op jit(solution)/shard_map/ppermute | solution.py:32
  66.4 1.6 %copy-start.1 = (f32[8,1,128,4,1,128]{5,4,3,2,1,0:T(1,128)S(1)}, f32[8,1,128,4,1,128]{5,4,3,2,1,0:T(1,128)}, u32[]{:S(2)}) copy-start(f32[8,1,128,4,1,128]{5,4,3,2,1,0:T(1,128)} %param.3) | copy-start | bytes 6291460

commit v3 on v2

--- a/solution.py
+++ b/solution.py
@@ -86,16 +86,15 @@
         send_ref[y] = total[pl.ds(pl.multiple_of((2 * y + 1 - core) * part, part), part), :]
 
 
-def inner_kernel(shift, piece_ref, y_ref, inner_ref):
+def inner_kernel(first_ref, second_ref, y_ref, inner_ref):
     row_tiles, nb, tile = y_ref.shape
-    part, cols = piece_ref.shape
-    col_tiles = cols // tile
-    half = part // 2
-    group = lax.axis_index("pcol") >> shift
-    inner = jnp.zeros((part, nb), F32)
-    for b in range(col_tiles):
-        left = split(piece_ref[:, b * tile : (b + 1) * tile])
-        inner += dot3(left, split(y_ref[b * (row_tiles // col_tiles) + group]), ((1,), (1,)))
+    ratio, half, cols = first_ref.shape
+    inner = jnp.zeros((2 * half, nb), F32)
+    for g in range(ratio):
+        for b in range(cols // tile):
+            at = slice(b * tile, (b + 1) * tile)
+            left = jnp.concatenate([first_ref[g, :, at], second_ref[g, :, at]], axis=0)
+            inner += dot3(split(left), split(y_ref[b * ratio + g]), ((1,), (1,)))
     for side in range(2):
         inner_ref[:, side * nb : (side + 1) * nb] = inner[side * half : (side + 1) * half]
 
@@ -249,7 +248,7 @@
         message = lax.dynamic_index_in_dim(kept, where["rounds"][r], 0, keepdims=False)
         turned.append(turn(message, 2 * r))
     turned = sum(turned[1:], turned[0])
-    kept = lax.optimization_barrier(kept)
+    y_piece, kept = lax.optimization_barrier((y_piece, kept))
     for mask in cols_order[:-1]:
         low, high = where["half"][mask]
         pair = kept.reshape(2, mask // 2, part, cols)
@@ -266,29 +265,30 @@
         cost_estimate=pl.CostEstimate(flops=6 * nb * nb * rows, bytes_accessed=rows * nb * 8, transcendentals=0),
     )(tfactor, y_rows)
     turned, u_rows = lax.optimization_barrier((turned, u_rows))
-    inner = pl.pallas_call(
-        functools.partial(inner_kernel, shift),
-        out_shape=shape(part // 2, 2 * nb),
-        in_specs=[whole] * 2,
-        out_specs=whole,
-        compiler_params=VMEM,
-        cost_estimate=pl.CostEstimate(flops=6 * nb * part * cols, bytes_accessed=cols * nb * 4, transcendentals=0),
-    )(turned, y_rows)
     first, second = turned[None, : part // 2], turned[None, part // 2 :]
     first, second = lax.optimization_barrier(first), lax.optimization_barrier(second)
     columns = jnp.concatenate([piece.reshape(2, part // 2, cols), y_cols])
     for mask in lead:
         first = join(first, swap(first, "pcol", mask), col[mask])
-        first, columns = lax.optimization_barrier((first, columns))
-        came = swap(jnp.concatenate([second, inner[None]]), "pcol", mask)
-        second, inner = join(second, came[:-1], col[mask]), inner + came[-1]
+        second = join(second, swap(second, "pcol", mask), col[mask])
+    first, columns = lax.optimization_barrier((first, columns))
+    first_group, second_group = first, second
     for mask in rest[:-2]:
         first = join(first, swap(first, "pcol", mask), col[mask])
         second = join(second, swap(second, "pcol", mask), col[mask])
     first = join(first, swap(first, "pcol", far), col[far])
     second = join(second, swap(second, "pcol", close), col[close])
-    first, inner = lax.optimization_barrier((first, inner))
-
+
+    columns = gather(columns, "prow", cols_order, row)
+    first, y_rows = lax.optimization_barrier((first, y_rows))
+    inner = pl.pallas_call(
+        inner_kernel,
+        out_shape=shape(part // 2, 2 * nb),
+        in_specs=[whole] * 3,
+        out_specs=whole,
+        compiler_params=VMEM,
+        cost_estimate=pl.CostEstimate(flops=6 * nb * part * cols, bytes_accessed=cols * nb * 4, transcendentals=0),
+    )(first_group, second_group, y_rows)
     for mask in cols_order[::-1]:
         inner = inner + swap(inner, "prow", mask)
     inner = inner[None]
@@ -298,7 +298,6 @@
     first = join(first, swap(first, "pcol", close), col[close])
     second = join(second, swap(second, "pcol", far), col[far])
 
-    columns = gather(columns, "prow", cols_order, row)
     u_cols, zc = pl.pallas_call(
         functools.partial(column_factor_kernel, cols_order),
         out_shape=[shape(3 * nb, cols, dtype=BF16), shape(nb, cols)],

time: 71.2 us -> 68.6 us (0.963)
  starting transfers between devices: 38.9 us -> 32.7 us
  waiting for transfers between devices: 20.9 us -> 24.9 us
    ppermute x21, waiting for transfers between devices: 20.9 us -> 24.9 us  [swap(): return lax.ppermute(values, axis, [(i, i ^ mask) for i in range(n)])]
    ppermute x21, starting transfers between devices: 33.7 us -> 30.2 us  [swap(): return lax.ppermute(values, axis, [(i, i ^ mask) for i in range(n)])]
    ppermute x3, starting transfers between devices: 5.16 us -> 2.46 us  [turn(): return lax.ppermute(values, BOTH, perm)]
  transfers between devices with their start and end apart: 24 -> 24, of which waited for: 16 -> 15; matrix products, arithmetic and copies ran while one was open for 1% -> 1% of each run, Pallas kernels for 3% -> 4%
where the time goes in v3:
time: 68.6 us; the launch traced here: 68.4 us
  starting transfers between devices  32.7 us (48%)
  waiting for transfers between devices  24.9 us (36%)
  Pallas kernels  6.69 us (10%)
  local copies, waits for them, and re-layouts  2.66 us (4%)
  other arithmetic  1.02 us (1%)
    ppermute x21, starting transfers between devices, swap(): return lax.ppermute(values, axis, [(i, i ^ mask) for i in range(n)])  30.2 us
    ppermute x21, waiting for transfers between devices, swap(): return lax.ppermute(values, axis, [(i, i ^ mask) for i in range(n)])  24.9 us
    pallas_call x1, Pallas kernels, per_device(): pl.pallas_call(functools.partial(update_kernel, orders, inner_upper), out...  2.98 us
    ppermute x3, starting transfers between devices, turn(): return lax.ppermute(values, BOTH, perm)  2.46 us
    unnamed x6, local copies, waits for them, and re-layouts  1.7 us
  transfers between devices with their start and end apart: 24, of which 15 were waited for; matrix products, arithmetic and copies ran while one was open for 1% of the time, Pallas kernels for 4%

profile of v3, /device:TPU:0, one launch (start us, length us, event | category | flops | bytes accessed | tf_op | source)
XLA Modules:
  0.0 68.4 jit_solution(14462751479496654838)
XLA Ops:
  0.0 0.9 %slice_bitcast_fusion.2 = (f32[1,4,32,128]{3,2,1,0:T(8,128)S(1)}, f32[1,4,32,128]{3,2,1,0:T(8,128)S(1)}) fusion(f32[8,32,128]{2,1,0:T(8,128)} %bitcast.153), kind=kLoop, calls=%fused_computation.51 | loop fusion | bytes 262144 | tf_op jit(solution)/shard_map/broadcast_in_dim | solution.py:223
  0.9 4.1 %collective-permute-start.1 = (f32[1,4,32,128]{3,2,1,0:T(8,128)S(1)}, f32[1,4,32,128]{3,2,1,0:T(8,128)S(1)}, u32[]{:S(2)}, u32[]{:S(2)}) collective-permute-start(f32[1,4,32,128]{3,2,1,0:T(8,128)S(1)} %get-tuple-element.97), channel_id=1, source_target_pairs={{0,4},{1,5},{2,6},{3,7},{4,0},{5,1},{6,2},{7,3},{8,12},{9,13},{10,... | collective-permute-start | bytes 196616 | tf_op jit(solution)/shard_map/ppermute | solution.py:32
  5.0 0.1 collective-permute-start
  5.1 1.6 %copy-done = f32[8,1,128,4,1,128]{5,4,3,2,1,0:T(1,128)S(1)} copy-done((f32[8,1,128,4,1,128]{5,4,3,2,1,0:T(1,128)S(1)}, f32[8,1,128,4,1,128]{5,4,3,2,1,0:T(1,128)}, u32[]{:S(2)}) %copy-start) | copy-done | bytes 2097176
  6.7 0.5 shard_map.37
  7.2 1.5 %collective-permute-done.1 = f32[1,4,32,128]{3,2,1,0:T(8,128)S(1)} collective-permute-done((f32[1,4,32,128]{3,2,1,0:T(8,128)S(1)}, f32[1,4,32,128]{3,2,1,0:T(8,128)S(1)}, u32[]{:S(2)}, u32[]{:S(2)}) %collective-permute-start.1) | collective-permute-done | bytes 65568 | tf_op jit(solution)/shard_map/ppermute | solution.py:32
  8.7 2.1 %collective-permute-start.2 = (f32[2,4,32,128]{3,2,1,0:T(8,128)S(1)}, f32[2,4,32,128]{3,2,1,0:T(8,128)S(1)}, u32[]{:S(2)}, u32[]{:S(2)}) collective-permute-start(f32[2,4,32,128]{3,2,1,0:T(8,128)S(1)} %maximum_bitcast_fusion.1), channel_id=1, source_target_pairs={{0,2},{1,3},{2,0},{3,1},{4,6},{5,7},{6,4},{7,5},{8,10},{9,11},{10,... | collective-permute-start | bytes 393224 | tf_op jit(solution)/shard_map/ppermute | solution.py:32
  10.8 0.6 collective-permute-done
  11.5 1.8 %collective-permute-start.4 = (f32[2,4,32,128]{3,2,1,0:T(8,128)S(1)}, f32[2,4,32,128]{3,2,1,0:T(8,128)S(1)}, u32[]{:S(2)}, u32[]{:S(2)}) collective-permute-start(f32[2,4,32,128]{3,2,1,0:T(8,128)S(1)} %maximum_bitcast_fusion.2), channel_id=1, source_target_pairs={{0,1},{1,0},{2,3},{3,2},{4,5},{5,4},{6,7},{7,6},{8,9},{9,8},{10,11... | collective-permute-start | bytes 393224 | tf_op jit(solution)/shard_map/ppermute | solution.py:32
  13.2 1.1 %collective-permute-done.2 = f32[2,4,32,128]{3,2,1,0:T(8,128)S(1)} collective-permute-done((f32[2,4,32,128]{3,2,1,0:T(8,128)S(1)}, f32[2,4,32,128]{3,2,1,0:T(8,128)S(1)}, u32[]{:S(2)}, u32[]{:S(2)}) %collective-permute-start.2) | collective-permute-done | bytes 131104 | tf_op jit(solution)/shard_map/ppermute | solution.py:32
  14.4 1.6 %collective-permute-start.3 = (f32[4,4,32,128]{3,2,1,0:T(8,128)S(1)}, f32[4,4,32,128]{3,2,1,0:T(8,128)S(1)}, u32[]{:S(2)}, u32[]{:S(2)}) collective-permute-start(f32[4,4,32,128]{3,2,1,0:T(8,128)S(1)} %bitcast.150), channel_id=1, source_target_pairs={{0,1},{1,0},{2,3},{3,2},{4,5},{5,4},{6,7},{7,6},{8,9},{9,8},{10,11... | collective-permute-start | bytes 786440 | tf_op jit(solution)/shard_map/ppermute | solution.py:32
  16.1 0.8 %collective-permute-done.4 = f32[2,4,32,128]{3,2,1,0:T(8,128)S(1)} collective-permute-done((f32[2,4,32,128]{3,2,1,0:T(8,128)S(1)}, f32[2,4,32,128]{3,2,1,0:T(8,128)S(1)}, u32[]{:S(2)}, u32[]{:S(2)}) %collective-permute-start.4) | collective-permute-done | bytes 131104 | tf_op jit(solution)/shard_map/ppermute | solution.py:32
  17.0 0.9 %collective-permute-start.5 = (f32[4,4,32,128]{3,2,1,0:T(8,128)S(1)}, f32[4,4,32,128]{3,2,1,0:T(8,128)S(1)}, u32[]{:S(2)}, u32[]{:S(2)}) collective-permute-start(f32[4,4,32,128]{3,2,1,0:T(8,128)S(1)} %bitcast.151), channel_id=1, source_target_pairs={{0,2},{1,3},{2,0},{3,1},{4,6},{5,7},{6,4},{7,5},{8,10},{9,11},{10,... | collective-permute-start | bytes 786440 | tf_op jit(solution)/shard_map/ppermute | solution.py:32
  17.9 4.5 %collective-permute-done.3 = f32[4,4,32,128]{3,2,1,0:T(8,128)S(1)} collective-permute-done((f32[4,4,32,128]{3,2,1,0:T(8,128)S(1)}, f32[4,4,32,128]{3,2,1,0:T(8,128)S(1)}, u32[]{:S(2)}, u32[]{:S(2)}) %collective-permute-start.3) | collective-permute-done | bytes 262176 | tf_op jit(solution)/shard_map/ppermute | solution.py:32
  22.3 1.6 %collective-permute-done.5 = f32[4,4,32,128]{3,2,1,0:T(8,128)S(1)} collective-permute-done((f32[4,4,32,128]{3,2,1,0:T(8,128)S(1)}, f32[4,4,32,128]{3,2,1,0:T(8,128)S(1)}, u32[]{:S(2)}, u32[]{:S(2)}) %collective-permute-start.5) | collective-permute-done | bytes 262176 | tf_op jit(solution)/shard_map/ppermute | solution.py:32
  23.9 0.1 select_bitcast_fusion.9
  24.2 0.0 copy-start.2
  24.2 1.1 %shard_map.38 = (f32[8,256,128]{2,1,0:T(8,128)S(1)}, f32[2,64,512]{2,1,0:T(8,128)S(1)}, f32[2,64,512]{2,1,0:T(8,128)S(1)}) custom-call(bf16[1024,512]{1,0:T(8,128)(2,1)S(1)} %get-tuple-element.38.ah_ref, bf16[1024,512]{1,0:T(8,128)(2,1)S(1)} %get-tuple-element.39.al_ref, f32[8,4,32,128]{3,2,1,0:T(8,128)S(1)} %bitcast.145, f32[8,4,32,128]{3,2,1,0:T(8,128)S(1)} %bitcast.144), custom_call_target="tpu_custom_call" | custom-call | flops 805306368 | bytes 4194304 | tf_op jit(solution)/shard_map/pallas_call | solution.py:230
  25.2 0.1 collective-permute-start.6
  25.4 1.5 %collective-permute-done.6 = f32[2,64,512]{2,1,0:T(8,128)S(1)} collective-permute-done((f32[2,64,512]{2,1,0:T(8,128)S(1)}, f32[2,64,512]{2,1,0:T(8,128)S(1)}, u32[]{:S(2)}, u32[]{:S(2)}) %collective-permute-start.6) | collective-permute-done | bytes 262176 | tf_op jit(solution)/shard_map/ppermute | solution.py:32
  26.9 1.1 %collective-permute-start.8 = (f32[64,512]{1,0:T(8,128)S(1)}, f32[64,512]{1,0:T(8,128)S(1)}, u32[]{:S(2)}, u32[]{:S(2)}) collective-permute-start(f32[64,512]{1,0:T(8,128)S(1)} %get-tuple-element.81), channel_id=1, source_target_pairs={{0,2},{1,10},{2,18},{3,26},{4,6},{5,14},{6,22},{7,30},{8,3},{9,11}... | collective-permute-start | bytes 393224 | tf_op jit(solution)/shard_map/ppermute | solution.py:210
  28.1 0.7 collective-permute-start.7
  28.7 0.0 copy-done.2
  28.7 1.0 %shard_map.39.ur_ref = bf16[1024,768]{1,0:T(8,128)(2,1)S(1)} custom-call(f32[256,256]{1,0:T(8,128)S(1)} %copy-done.2, f32[8,256,128]{2,1,0:T(8,128)S(1)} %get-tuple-element.64.y_ref), custom_call_target="tpu_custom_call" | custom-call | flops 402653184 | bytes 2097152 | tf_op jit(solution)/shard_map/pallas_call | solution.py:259
  29.8 4.3 %collective-permute-start.10 = (f32[1,64,512]{2,1,0:T(8,128)S(1)}, f32[1,64,512]{2,1,0:T(8,128)S(1)}, u32[]{:S(2)}, u32[]{:S(2)}) collective-permute-start(f32[1,64,512]{2,1,0:T(8,128)S(1)} %constant_dynamic-slice_fusion), channel_id=1, source_target_pairs={{0,16},{8,24},{16,0},{24,8},{1,17},{9,25},{17,1},{25,9},{2,18},{10... | collective-permute-start | bytes 393224 | tf_op jit(solution)/shard_map/ppermute | solution.py:32
  34.1 0.7 collective-permute-start.11
  34.8 0.0 collective-permute-done.8
  34.8 0.0 collective-permute-done.7
  34.8 3.4 %collective-permute-start.9 = (f32[1,32,512]{2,1,0:T(8,128)S(1)}, f32[1,32,512]{2,1,0:T(8,128)S(1)}, u32[]{:S(2)}, u32[]{:S(2)}) collective-permute-start(f32[1,32,512]{2,1,0:T(8,128)S(1)} %get-tuple-element.90), channel_id=1, source_target_pairs={{0,4},{1,5},{2,6},{3,7},{4,0},{5,1},{6,2},{7,3},{8,12},{9,13},{10,... | collective-permute-start | bytes 196616 | tf_op jit(solution)/shard_map/ppermute | solution.py:32
  38.3 0.1 collective-permute-start.16
  38.4 3.7 %collective-permute-done.10 = f32[1,64,512]{2,1,0:T(8,128)S(1)} collective-permute-done((f32[1,64,512]{2,1,0:T(8,128)S(1)}, f32[1,64,512]{2,1,0:T(8,128)S(1)}, u32[]{:S(2)}, u32[]{:S(2)}) %collective-permute-start.10) | collective-permute-done | bytes 131104 | tf_op jit(solution)/shard_map/ppermute | solution.py:32
  42.1 0.0 collective-permute-done.11
  42.1 0.0 collective-permute-done.9
  42.2 4.1 %collective-permute-start.14 = (f32[2,32,512]{2,1,0:T(8,128)S(1)}, f32[2,32,512]{2,1,0:T(8,128)S(1)}, u32[]{:S(2)}, u32[]{:S(2)}) collective-permute-start(f32[2,32,512]{2,1,0:T(8,128)S(1)} %maximum_bitcast_fusion.3.first_ref), channel_id=1, source_target_pairs={{0,2},{1,3},{2,0},{3,1},{4,6},{5,7},{6,4},{7,5},{8,10},{9,11},{10,... | collective-permute-start | bytes 393224 | tf_op jit(solution)/shard_map/ppermute | solution.py:32
  46.3 0.0 collective-permute-done.16
  46.3 1.4 %collective-permute-start.17 = (f32[2,32,512]{2,1,0:T(8,128)S(1)}, f32[2,32,512]{2,1,0:T(8,128)S(1)}, u32[]{:S(2)}, u32[]{:S(2)}) collective-permute-start(f32[2,32,512]{2,1,0:T(8,128)S(1)} %maximum_bitcast_fusion.4.second_ref), channel_id=1, source_target_pairs={{0,1},{1,0},{2,3},{3,2},{4,5},{5,4},{6,7},{7,6},{8,9},{9,8},{10,11... | collective-permute-start | bytes 393224 | tf_op jit(solution)/shard_map/ppermute | solution.py:32
  47.7 0.4 collective-permute-start.12
  48.2 2.5 %collective-permute-done.14 = f32[2,32,512]{2,1,0:T(8,128)S(1)} collective-permute-done((f32[2,32,512]{2,1,0:T(8,128)S(1)}, f32[2,32,512]{2,1,0:T(8,128)S(1)}, u32[]{:S(2)}, u32[]{:S(2)}) %collective-permute-start.14) | collective-permute-done | bytes 131104 | tf_op jit(solution)/shard_map/ppermute | solution.py:32
  50.7 0.7 shard_map.41
  51.3 0.1 collective-permute-start.19
  51.4 0.1 collective-permute-start.15
  51.5 0.8 %collective-permute-done.17 = f32[2,32,512]{2,1,0:T(8,128)S(1)} collective-permute-done((f32[2,32,512]{2,1,0:T(8,128)S(1)}, f32[2,32,512]{2,1,0:T(8,128)S(1)}, u32[]{:S(2)}, u32[]{:S(2)}) %collective-permute-start.17) | collective-permute-done | bytes 131104 | tf_op jit(solution)/shard_map/ppermute | solution.py:32
  52.4 0.3 collective-permute-done.19
  52.7 1.6 %collective-permute-start.20 = (f32[32,512]{1,0:T(8,128)S(1)}, f32[32,512]{1,0:T(8,128)S(1)}, u32[]{:S(2)}, u32[]{:S(2)}) collective-permute-start(f32[32,512]{1,0:T(8,128)S(1)} %add.44), channel_id=1, source_target_pairs={{0,16},{8,24},{16,0},{24,8},{1,17},{9,25},{17,1},{25,9},{2,18},{10... | collective-permute-start | bytes 196616 | tf_op jit(solution)/shard_map/ppermute | solution.py:32
  54.3 0.4 collective-permute-start.18
  54.7 2.9 %collective-permute-done.20 = f32[32,512]{1,0:T(8,128)S(1)} collective-permute-done((f32[32,512]{1,0:T(8,128)S(1)}, f32[32,512]{1,0:T(8,128)S(1)}, u32[]{:S(2)}, u32[]{:S(2)}) %collective-permute-start.20) | collective-permute-done | bytes 65568 | tf_op jit(solution)/shard_map/ppermute | solution.py:32
  57.6 1.1 %collective-permute-start.23 = (f32[1,32,512]{2,1,0:T(8,128)S(1)}, f32[1,32,512]{2,1,0:T(8,128)S(1)}, u32[]{:S(2)}, u32[]{:S(2)}) collective-permute-start(f32[1,32,512]{2,1,0:T(8,128)S(1)} %add_bitcast_fusion.refs_0_), channel_id=1, source_target_pairs={{0,3},{1,2},{2,1},{3,0},{4,7},{5,6},{6,5},{7,4},{8,11},{9,10},{10,... | collective-permute-start | bytes 196616 | tf_op jit(solution)/shard_map/ppermute | solution.py:32
  58.8 1.6 %collective-permute-start.22 = (f32[1,32,512]{2,1,0:T(8,128)S(1)}, f32[1,32,512]{2,1,0:T(8,128)S(1)}, u32[]{:S(2)}, u32[]{:S(2)}) collective-permute-start(f32[1,32,512]{2,1,0:T(8,128)S(1)} %add_bitcast_fusion.refs_0_), channel_id=1, source_target_pairs={{0,2},{1,3},{2,0},{3,1},{4,6},{5,7},{6,4},{7,5},{8,10},{9,11},{10,... | collective-permute-start | bytes 196616 | tf_op jit(solution)/shard_map/ppermute | solution.py:32
  60.3 0.0 collective-permute-done.12
  60.3 0.8 %collective-permute-start.21 = (f32[1,32,512]{2,1,0:T(8,128)S(1)}, f32[1,32,512]{2,1,0:T(8,128)S(1)}, u32[]{:S(2)}, u32[]{:S(2)}) collective-permute-start(f32[1,32,512]{2,1,0:T(8,128)S(1)} %add_bitcast_fusion.refs_0_), channel_id=1, source_target_pairs={{0,1},{1,0},{2,3},{3,2},{4,5},{5,4},{6,7},{7,6},{8,9},{9,8},{10,11... | collective-permute-start | bytes 196616 | tf_op jit(solution)/shard_map/ppermute | solution.py:32
  61.3 0.0 collective-permute-done.15
  61.3 0.1 collective-permute-start.13
  61.4 2.1 %collective-permute-done.18 = f32[4,32,512]{2,1,0:T(8,128)S(1)} collective-permute-done((f32[4,32,512]{2,1,0:T(8,128)S(1)}, f32[4,32,512]{2,1,0:T(8,128)S(1)}, u32[]{:S(2)}, u32[]{:S(2)}) %collective-permute-start.18) | collective-permute-done | bytes 262176 | tf_op jit(solution)/shard_map/ppermute | solution.py:32
  63.6 0.1 select_bitcast_fusion.3
  63.7 0.0 collective-permute-done.13
  63.7 0.1 select_bitcast_fusion.1
  63.8 0.0 copy-start.1
  63.8 0.1 pad_maximum_fusion
  63.9 0.4 shard_map.40
  64.4 0.7 collective-permute-done.23.refs_3_
  65.0 0.3 collective-permute-done.22.refs_2_
  65.3 0.0 collective-permute-done.21.refs_1_
  65.3 0.1 copy-done.1
  65.4 3.0 %shard_map.42 = f32[4096,128]{1,0:T(8,128)} custom-call(f32[4096,128]{1,0:T(8,128)S(1)} %bitcast.139, bf16[1024,768]{1,0:T(8,128)(2,1)S(1)} %shard_map.39.ur_ref, bf16[768,512]{1,0:T(8,128)(2,1)S(1)} %get-tuple-element.60.uc_ref, f32[256,512]{1,0:T(8,128)S(1)} %get-tuple-element.61.zc_ref, f32[8,32,512]{2,1,0:T(8,128)S(1)} %bitcast.142, ...), custom_call_target="tpu_custom_call" | custom-call | flops 1610612736 | bytes 4194304 | tf_op jit(solution)/shard_map/pallas_call | solution.py:314
  (34 shorter events, 0.7 us)
Async XLA Ops:
  0.9 7.8 %collective-permute-start.1 = (f32[1,4,32,128]{3,2,1,0:T(8,128)S(1)}, f32[1,4,32,128]{3,2,1,0:T(8,128)S(1)}, u32[]{:S(2)}, u32[]{:S(2)}) collective-permute-start(f32[1,4,32,128]{3,2,1,0:T(8,128)S(1)} %get-tuple-element.97), channel_id=1, source_target_pairs={{0,4},{1,5},{2,6},{3,7},{4,0},{5,1},{6,2},{7,3},{8,12},{9,13},{10,... | collective-permute-start | bytes 196616 | tf_op jit(solution)/shard_map/ppermute | solution.py:32
  5.0 6.5 %collective-permute-start = (f32[1,4,32,128]{3,2,1,0:T(8,128)S(1)}, f32[1,4,32,128]{3,2,1,0:T(8,128)S(1)}, u32[]{:S(2)}, u32[]{:S(2)}) collective-permute-start(f32[1,4,32,128]{3,2,1,0:T(8,128)S(1)} %get-tuple-element.98), channel_id=1, source_target_pairs={{0,4},{1,5},{2,6},{3,7},{4,0},{5,1},{6,2},{7,3},{8,12},{9,13},{10,... | collective-permute-start | bytes 196616 | tf_op jit(solution)/shard_map/ppermute | solution.py:32
  5.1 1.6 %copy-start = (f32[8,1,128,4,1,128]{5,4,3,2,1,0:T(1,128)S(1)}, f32[8,1,128,4,1,128]{5,4,3,2,1,0:T(1,128)}, u32[]{:S(2)}) copy-start(f32[8,1,128,4,1,128]{5,4,3,2,1,0:T(1,128)} %param.3) | copy-start | bytes 6291460
  8.7 5.7 %collective-permute-start.2 = (f32[2,4,32,128]{3,2,1,0:T(8,128)S(1)}, f32[2,4,32,128]{3,2,1,0:T(8,128)S(1)}, u32[]{:S(2)}, u32[]{:S(2)}) collective-permute-start(f32[2,4,32,128]{3,2,1,0:T(8,128)S(1)} %maximum_bitcast_fusion.1), channel_id=1, source_target_pairs={{0,2},{1,3},{2,0},{3,1},{4,6},{5,7},{6,4},{7,5},{8,10},{9,11},{10,... | collective-permute-start | bytes 393224 | tf_op jit(solution)/shard_map/ppermute | solution.py:32
  11.5 5.4 %collective-permute-start.4 = (f32[2,4,32,128]{3,2,1,0:T(8,128)S(1)}, f32[2,4,32,128]{3,2,1,0:T(8,128)S(1)}, u32[]{:S(2)}, u32[]{:S(2)}) collective-permute-start(f32[2,4,32,128]{3,2,1,0:T(8,128)S(1)} %maximum_bitcast_fusion.2), channel_id=1, source_target_pairs={{0,1},{1,0},{2,3},{3,2},{4,5},{5,4},{6,7},{7,6},{8,9},{9,8},{10,11... | collective-permute-start | bytes 393224 | tf_op jit(solution)/shard_map/ppermute | solution.py:32
  14.4 7.9 %collective-permute-start.3 = (f32[4,4,32,128]{3,2,1,0:T(8,128)S(1)}, f32[4,4,32,128]{3,2,1,0:T(8,128)S(1)}, u32[]{:S(2)}, u32[]{:S(2)}) collective-permute-start(f32[4,4,32,128]{3,2,1,0:T(8,128)S(1)} %bitcast.150), channel_id=1, source_target_pairs={{0,1},{1,0},{2,3},{3,2},{4,5},{5,4},{6,7},{7,6},{8,9},{9,8},{10,11... | collective-permute-start | bytes 786440 | tf_op jit(solution)/shard_map/ppermute | solution.py:32
  17.0 7.0 %collective-permute-start.5 = (f32[4,4,32,128]{3,2,1,0:T(8,128)S(1)}, f32[4,4,32,128]{3,2,1,0:T(8,128)S(1)}, u32[]{:S(2)}, u32[]{:S(2)}) collective-permute-start(f32[4,4,32,128]{3,2,1,0:T(8,128)S(1)} %bitcast.151), channel_id=1, source_target_pairs={{0,2},{1,3},{2,0},{3,1},{4,6},{5,7},{6,4},{7,5},{8,10},{9,11},{10,... | collective-permute-start | bytes 786440 | tf_op jit(solution)/shard_map/ppermute | solution.py:32
  24.2 4.6 %copy-start.2 = (f32[256,256]{1,0:T(8,128)S(1)}, f32[256,256]{1,0:T(8,128)}, u32[]{:S(2)}) copy-start(f32[256,256]{1,0:T(8,128)} %t_ref.3) | copy-start | bytes 786436
  25.2 1.6 %collective-permute-start.6 = (f32[2,64,512]{2,1,0:T(8,128)S(1)}, f32[2,64,512]{2,1,0:T(8,128)S(1)}, u32[]{:S(2)}, u32[]{:S(2)}) collective-permute-start(f32[2,64,512]{2,1,0:T(8,128)S(1)} %get-tuple-element.45), channel_id=1, source_target_pairs={{0,8},{8,0},{16,24},{24,16},{1,9},{9,1},{17,25},{25,17},{2,10},{10... | collective-permute-start | bytes 786440 | tf_op jit(solution)/shard_map/ppermute | solution.py:32
  26.9 7.8 %collective-permute-start.8 = (f32[64,512]{1,0:T(8,128)S(1)}, f32[64,512]{1,0:T(8,128)S(1)}, u32[]{:S(2)}, u32[]{:S(2)}) collective-permute-start(f32[64,512]{1,0:T(8,128)S(1)} %get-tuple-element.81), channel_id=1, source_target_pairs={{0,2},{1,10},{2,18},{3,26},{4,6},{5,14},{6,22},{7,30},{8,3},{9,11}... | collective-permute-start | bytes 393224 | tf_op jit(solution)/shard_map/ppermute | solution.py:210
  28.1 6.7 %collective-permute-start.7 = (f32[64,512]{1,0:T(8,128)S(1)}, f32[64,512]{1,0:T(8,128)S(1)}, u32[]{:S(2)}, u32[]{:S(2)}) collective-permute-start(f32[64,512]{1,0:T(8,128)S(1)} %get-tuple-element.82), channel_id=1, source_target_pairs={{0,0},{1,8},{2,16},{3,24},{4,4},{5,12},{6,20},{7,28},{8,1},{9,9},{... | collective-permute-start | bytes 393224 | tf_op jit(solution)/shard_map/ppermute | solution.py:210
  29.8 12.2 %collective-permute-start.10 = (f32[1,64,512]{2,1,0:T(8,128)S(1)}, f32[1,64,512]{2,1,0:T(8,128)S(1)}, u32[]{:S(2)}, u32[]{:S(2)}) collective-permute-start(f32[1,64,512]{2,1,0:T(8,128)S(1)} %constant_dynamic-slice_fusion), channel_id=1, source_target_pairs={{0,16},{8,24},{16,0},{24,8},{1,17},{9,25},{17,1},{25,9},{2,18},{10... | collective-permute-start | bytes 393224 | tf_op jit(solution)/shard_map/ppermute | solution.py:32
  34.1 8.0 %collective-permute-start.11 = (f32[64,512]{1,0:T(8,128)S(1)}, f32[64,512]{1,0:T(8,128)S(1)}, u32[]{:S(2)}, u32[]{:S(2)}) collective-permute-start(f32[64,512]{1,0:T(8,128)S(1)} %copy_bitcast_fusion), channel_id=1, source_target_pairs={{0,0},{1,8},{2,16},{3,24},{4,4},{5,12},{6,20},{7,28},{8,1},{9,9},{... | collective-permute-start | bytes 393224 | tf_op jit(solution)/shard_map/ppermute | solution.py:210
  34.8 7.3 %collective-permute-start.9 = (f32[1,32,512]{2,1,0:T(8,128)S(1)}, f32[1,32,512]{2,1,0:T(8,128)S(1)}, u32[]{:S(2)}, u32[]{:S(2)}) collective-permute-start(f32[1,32,512]{2,1,0:T(8,128)S(1)} %get-tuple-element.90), channel_id=1, source_target_pairs={{0,4},{1,5},{2,6},{3,7},{4,0},{5,1},{6,2},{7,3},{8,12},{9,13},{10,... | collective-permute-start | bytes 196616 | tf_op jit(solution)/shard_map/ppermute | solution.py:32
  38.3 8.0 %collective-permute-start.16 = (f32[1,32,512]{2,1,0:T(8,128)S(1)}, f32[1,32,512]{2,1,0:T(8,128)S(1)}, u32[]{:S(2)}, u32[]{:S(2)}) collective-permute-start(f32[1,32,512]{2,1,0:T(8,128)S(1)} %get-tuple-element.89), channel_id=1, source_target_pairs={{0,4},{1,5},{2,6},{3,7},{4,0},{5,1},{6,2},{7,3},{8,12},{9,13},{10,... | collective-permute-start | bytes 196616 | tf_op jit(solution)/shard_map/ppermute | solution.py:32
  42.2 8.4 %collective-permute-start.14 = (f32[2,32,512]{2,1,0:T(8,128)S(1)}, f32[2,32,512]{2,1,0:T(8,128)S(1)}, u32[]{:S(2)}, u32[]{:S(2)}) collective-permute-start(f32[2,32,512]{2,1,0:T(8,128)S(1)} %maximum_bitcast_fusion.3.first_ref), channel_id=1, source_target_pairs={{0,2},{1,3},{2,0},{3,1},{4,6},{5,7},{6,4},{7,5},{8,10},{9,11},{10,... | collective-permute-start | bytes 393224 | tf_op jit(solution)/shard_map/ppermute | solution.py:32
  46.3 6.0 %collective-permute-start.17 = (f32[2,32,512]{2,1,0:T(8,128)S(1)}, f32[2,32,512]{2,1,0:T(8,128)S(1)}, u32[]{:S(2)}, u32[]{:S(2)}) collective-permute-start(f32[2,32,512]{2,1,0:T(8,128)S(1)} %maximum_bitcast_fusion.4.second_ref), channel_id=1, source_target_pairs={{0,1},{1,0},{2,3},{3,2},{4,5},{5,4},{6,7},{7,6},{8,9},{9,8},{10,11... | collective-permute-start | bytes 393224 | tf_op jit(solution)/shard_map/ppermute | solution.py:32
  47.7 12.6 %collective-permute-start.12 = (f32[1,4,32,512]{3,2,1,0:T(8,128)S(1)}, f32[1,4,32,512]{3,2,1,0:T(8,128)S(1)}, u32[]{:S(2)}, u32[]{:S(2)}) collective-permute-start(f32[1,4,32,512]{3,2,1,0:T(8,128)S(1)} %bitcast.146), channel_id=1, source_target_pairs={{0,16},{8,24},{16,0},{24,8},{1,17},{9,25},{17,1},{25,9},{2,18},{10... | collective-permute-start | bytes 786440 | tf_op jit(solution)/shard_map/ppermute | solution.py:32
  51.3 1.3 %collective-permute-start.19 = (f32[32,512]{1,0:T(8,128)S(1)}, f32[32,512]{1,0:T(8,128)S(1)}, u32[]{:S(2)}, u32[]{:S(2)}) collective-permute-start(f32[32,512]{1,0:T(8,128)S(1)} %shard_map.41), channel_id=1, source_target_pairs={{0,8},{8,0},{16,24},{24,16},{1,9},{9,1},{17,25},{25,17},{2,10},{10... | collective-permute-start | bytes 196616 | tf_op jit(solution)/shard_map/ppermute | solution.py:32
  51.4 9.9 %collective-permute-start.15 = (f32[4,32,512]{2,1,0:T(8,128)S(1)}, f32[4,32,512]{2,1,0:T(8,128)S(1)}, u32[]{:S(2)}, u32[]{:S(2)}) collective-permute-start(f32[4,32,512]{2,1,0:T(8,128)S(1)} %bitcast.147), channel_id=1, source_target_pairs={{0,1},{1,0},{2,3},{3,2},{4,5},{5,4},{6,7},{7,6},{8,9},{9,8},{10,11... | collective-permute-start | bytes 786440 | tf_op jit(solution)/shard_map/ppermute | solution.py:32
  52.7 4.9 %collective-permute-start.20 = (f32[32,512]{1,0:T(8,128)S(1)}, f32[32,512]{1,0:T(8,128)S(1)}, u32[]{:S(2)}, u32[]{:S(2)}) collective-permute-start(f32[32,512]{1,0:T(8,128)S(1)} %add.44), channel_id=1, source_target_pairs={{0,16},{8,24},{16,0},{24,8},{1,17},{9,25},{17,1},{25,9},{2,18},{10... | collective-permute-start | bytes 196616 | tf_op jit(solution)/shard_map/ppermute | solution.py:32
  54.3 9.3 %collective-permute-start.18 = (f32[4,32,512]{2,1,0:T(8,128)S(1)}, f32[4,32,512]{2,1,0:T(8,128)S(1)}, u32[]{:S(2)}, u32[]{:S(2)}) collective-permute-start(f32[4,32,512]{2,1,0:T(8,128)S(1)} %bitcast.149), channel_id=1, source_target_pairs={{0,2},{1,3},{2,0},{3,1},{4,6},{5,7},{6,4},{7,5},{8,10},{9,11},{10,... | collective-permute-start | bytes 786440 | tf_op jit(solution)/shard_map/ppermute | solution.py:32
  57.6 7.4 %collective-permute-start.23 = (f32[1,32,512]{2,1,0:T(8,128)S(1)}, f32[1,32,512]{2,1,0:T(8,128)S(1)}, u32[]{:S(2)}, u32[]{:S(2)}) collective-permute-start(f32[1,32,512]{2,1,0:T(8,128)S(1)} %add_bitcast_fusion.refs_0_), channel_id=1, source_target_pairs={{0,3},{1,2},{2,1},{3,0},{4,7},{5,6},{6,5},{7,4},{8,11},{9,10},{10,... | collective-permute-start | bytes 196616 | tf_op jit(solution)/shard_map/ppermute | solution.py:32
  58.8 6.5 %collective-permute-start.22 = (f32[1,32,512]{2,1,0:T(8,128)S(1)}, f32[1,32,512]{2,1,0:T(8,128)S(1)}, u32[]{:S(2)}, u32[]{:S(2)}) collective-permute-start(f32[1,32,512]{2,1,0:T(8,128)S(1)} %add_bitcast_fusion.refs_0_), channel_id=1, source_target_pairs={{0,2},{1,3},{2,0},{3,1},{4,6},{5,7},{6,4},{7,5},{8,10},{9,11},{10,... | collective-permute-start | bytes 196616 | tf_op jit(solution)/shard_map/ppermute | solution.py:32
  60.3 5.0 %collective-permute-start.21 = (f32[1,32,512]{2,1,0:T(8,128)S(1)}, f32[1,32,512]{2,1,0:T(8,128)S(1)}, u32[]{:S(2)}, u32[]{:S(2)}) collective-permute-start(f32[1,32,512]{2,1,0:T(8,128)S(1)} %add_bitcast_fusion.refs_0_), channel_id=1, source_target_pairs={{0,1},{1,0},{2,3},{3,2},{4,5},{5,4},{6,7},{7,6},{8,9},{9,8},{10,11... | collective-permute-start | bytes 196616 | tf_op jit(solution)/shard_map/ppermute | solution.py:32
  61.3 2.4 %collective-permute-start.13 = (f32[2,4,32,512]{3,2,1,0:T(8,128)S(1)}, f32[2,4,32,512]{3,2,1,0:T(8,128)S(1)}, u32[]{:S(2)}, u32[]{:S(2)}) collective-permute-start(f32[2,4,32,512]{3,2,1,0:T(8,128)S(1)} %maximum_bitcast_fusion), channel_id=1, source_target_pairs={{0,8},{8,0},{16,24},{24,16},{1,9},{9,1},{17,25},{25,17},{2,10},{10... | collective-permute-start | bytes 1572872 | tf_op jit(solution)/shard_map/ppermute | solution.py:32
  63.8 1.6 %copy-start.1 = (f32[8,1,128,4,1,128]{5,4,3,2,1,0:T(1,128)S(1)}, f32[8,1,128,4,1,128]{5,4,3,2,1,0:T(1,128)}, u32[]{:S(2)}) copy-start(f32[8,1,128,4,1,128]{5,4,3,2,1,0:T(1,128)} %param.3) | copy-start | bytes 6291460
